TPU v7x, 32 devices: a whole 2x2x4 slice. The times are simulated.
32 devices in a mesh: segment: 4 (over x, core), patch: 8 (over z, y).
Axes of the slice: x: 2, y: 2, z: 4, core: 2. Of those that a mesh axis runs over, the one named last changes fastest.
Arguments:
- features: bfloat16 [32, 28, 4, 12, 128], P('patch'), may hold values from -6 to 6
- deep_path: bfloat16 [32, 28, 4, 12, 128], P('patch'), may hold values from -6 to 6
- weight_first: bfloat16 [9, 28, 28], replicated, may hold values from -0.375 to 0.375
- bias_first: float32 [28], replicated, may hold values from -3 to 3
- weight_second: bfloat16 [27, 28, 28], replicated, may hold values from -0.21875 to 0.21875
- bias_second: float32 [28], replicated, may hold values from -3 to 3
- weight_third: bfloat16 [27, 28, 56], replicated, may hold values from -0.15625 to 0.15625
- bias_third: float32 [28], replicated, may hold values from -3 to 3
- weight_fourth: bfloat16 [27, 28, 56], replicated, may hold values from -0.15625 to 0.15625
- bias_fourth: float32 [28], replicated, may hold values from -3 to 3
- head_weight: bfloat16 [3, 28], replicated, may hold values from -2 to 2
- head_bias: float32 [3], replicated, may hold values from -3 to 3
- block_first: int32 [32], replicated, may hold values from 0 to 60, as said below
- block_offset: int32 [32], replicated, may hold values from 0 to 3
Outputs:
- blended: float32 [8, 8, 3, 4, 4, 128], P(None, 'patch', None, 'segment')
Inputs may be any that keep to these rules, and one draw needn't show every extreme that they name: A patch touches only blocks block_first to block_first + 3, all inside the slab.
All inputs are finite; a program needn't handle non-finite values.
Results may differ from a plain program's by a relative error of at most 0.0022.
Values may be sent and summed in bfloat16 or wider, within the bound.
No kernel may reach another device: no remote copies, remote signals or barrier semaphores. Data moves between devices by JAX's collectives and lax.ppermute only.
A program may use at most 64 MiB of HBM per device.

v0:
```python
import jax
import jax.numpy as jnp
from jax import lax
from jax.sharding import PartitionSpec as P

CW = 4
CH_DEV = 8
KMAX = 4


def extended(array, sides, width):
    for axis, dim in sides:
        size, length = (lax.axis_size(axis), array.shape[dim])
        up = [(i, (i + 1) % size) for i in range(size - 1)]
        down = [(j, i) for i, j in up]
        last = lax.slice_in_dim(array, length - width, length, axis=dim)
        first = lax.slice_in_dim(array, 0, width, axis=dim)
        before = lax.ppermute(last, axis, up)
        after = lax.ppermute(first, axis, down)
        array = jnp.concatenate([before, array, after], axis=dim)
    return array


def bump(count):
    place = (jnp.arange(count).astype(jnp.float32) + 0.5) / count
    return jnp.sin(jnp.pi * place) ** 2


def blend_window(depth, along, across):
    return bump(depth)[:, None, None] * bump(along)[None, :, None] * bump(across)[None, None, :]


def convolve_plane(source, kernel):
    depth, along, across = (source.shape[1], source.shape[2], source.shape[3])
    padded = jnp.pad(source, ((0, 0), (0, 0), (1, 1), (1, 1)))
    total = jnp.zeros((kernel.shape[1], depth, along, across), jnp.float32)
    for row_shift in range(3):
        for col_shift in range(3):
            window = padded[:, :, row_shift : row_shift + along, col_shift : col_shift + across]
            total = total + jnp.einsum(
                "oc,czay->ozay",
                kernel[row_shift * 3 + col_shift],
                window,
                preferred_element_type=jnp.float32,
            )
    return total


def convolve_inner(source, kernel):
    depth, along, across = (source.shape[1] - 2, source.shape[2], source.shape[3])
    padded = jnp.pad(source, ((0, 0), (0, 0), (1, 1), (1, 1)))
    total = jnp.zeros((kernel.shape[1], depth, along, across), jnp.float32)
    for depth_shift in range(3):
        for row_shift in range(3):
            for col_shift in range(3):
                window = padded[
                    :,
                    depth_shift : depth_shift + depth,
                    row_shift : row_shift + along,
                    col_shift : col_shift + across,
                ]
                total = total + jnp.einsum(
                    "oc,czay->ozay",
                    kernel[depth_shift * 9 + row_shift * 3 + col_shift],
                    window,
                    preferred_element_type=jnp.float32,
                )
    return total


def layer(total, bias):
    return jax.nn.relu(total + bias[:, None, None, None]).astype(jnp.bfloat16)


def per_device(
    features,
    deep_path,
    weight_first,
    bias_first,
    weight_second,
    bias_second,
    weight_third,
    bias_third,
    weight_fourth,
    bias_fourth,
    head_weight,
    head_bias,
    block_first,
    block_offset,
):
    segment_index = lax.axis_index("segment")
    owner = lax.axis_index("patch")
    segments = lax.axis_size("segment")
    owners = lax.axis_size("patch")
    count_all = features.shape[0]
    depth, along, across = (features.shape[2], features.shape[3], features.shape[4])
    quarter = depth // segments
    window_all = blend_window(depth, along, across)
    lower = segment_index * quarter
    local_in = lax.dynamic_slice_in_dim(features, lower, quarter, 2)
    local_deep = lax.dynamic_slice_in_dim(deep_path, lower, quarter, 2)

    def rimmed(values):
        return extended(values, (("segment", 2),), 1)

    first = jax.vmap(lambda item: layer(convolve_plane(item, weight_first), bias_first))(local_in)
    second = jax.vmap(lambda item: layer(convolve_inner(item, weight_second), bias_second))(
        rimmed(first)
    )
    third = jax.vmap(lambda item: layer(convolve_inner(item, weight_third), bias_third))(
        rimmed(jnp.concatenate([second, local_deep], axis=1))
    )
    settled = jax.vmap(lambda item: layer(convolve_inner(item, weight_fourth), bias_fourth))(
        rimmed(jnp.concatenate([third, first], axis=1))
    )
    window = lax.dynamic_slice_in_dim(window_all, lower, quarter, 0)
    own_first = lax.dynamic_slice_in_dim(block_first, owner * count_all, count_all)
    own_offset = lax.dynamic_slice_in_dim(block_offset, owner * count_all, count_all)
    logits = jnp.einsum("oc,mczay->mozay", head_weight, settled, preferred_element_type=jnp.float32)
    logits = logits + head_bias[None, :, None, None, None]
    partial_value = jax.nn.sigmoid(logits) * window[None, None]
    held = partial_value.shape[2]

    def place(part_one, first_block, offset):
        canvas = jnp.zeros((3, held, KMAX * CW, across), jnp.float32)
        zero = jnp.zeros((), jnp.int32)
        canvas = lax.dynamic_update_slice(canvas, part_one, (zero, zero, offset, zero))
        pieces = canvas.reshape(3, held, KMAX, CW, across)
        filler = jnp.zeros((3, held, owners - KMAX, CW, across), jnp.float32)
        pieces = jnp.concatenate([pieces, filler], axis=2)
        order = (jnp.arange(owners, dtype=jnp.int32) - first_block) % owners
        return jnp.take(pieces, order, axis=2)

    slots = jax.vmap(place)(partial_value, own_first, own_offset)
    slots = slots.transpose(3, 0, 1, 2, 4, 5)
    mine = lax.all_to_all(slots, "patch", split_axis=0, concat_axis=0, tiled=True)
    mine_flat = mine.reshape(owners * count_all, 3 * quarter * CW * across)
    advance = (owner - block_first) % owners
    chosen = block_first + advance
    usable = advance < KMAX
    local_index = chosen // owners
    onehot = (
        (local_index[None, :] == jnp.arange(CH_DEV, dtype=jnp.int32)[:, None]) & usable[None, :]
    ).astype(jnp.float32)
    blended = jnp.dot(
        onehot, mine_flat, precision=lax.Precision.HIGHEST, preferred_element_type=jnp.float32
    )
    return blended.reshape(CH_DEV, 1, 3, quarter, CW, across)


def solution(mesh):
    placed = (
        P("patch", None, None, None, None),
        P("patch", None, None, None, None),
        P(),
        P(),
        P(),
        P(),
        P(),
        P(),
        P(),
        P(),
        P(),
        P(),
        P(),
        P(),
    )
    return jax.shard_map(
        per_device,
        mesh=mesh,
        in_specs=placed,
        out_specs=P(None, "patch", None, "segment", None, None),
        check_vma=False,
    )
```

profile of v0, /device:TPU:1, one launch (start us, length us, event | category | flops | bytes accessed | tf_op | source)
XLA Modules:
  0.0 143.8 jit_solution(9992323544557944358)
XLA Ops:
  0.0 1.3 copy-done
  2.1 1.0 fusion.162
  3.2 0.9 convolution_add_fusion.13
  6.3 4.5 %collective-permute-start = (bf16[4,28,1,12,128]{4,1,3,0,2:T(8,128)(2,1)S(1)}, bf16[4,28,1,12,128]{4,1,3,0,2:T(8,128)(2,1)S(1)}, u32[]{:S(2)}, u32[]{:S(2)}) collective-permute-start(bf16[4,28,1,12,128]{4,1,3,0,2:T(8,128)(2,1)S(1)} %bitcast.1360), channel_id=1, source_target_pairs={{0,8},{8,16},{16,24},{1,9},{9,17},{17,25},{2,10},{10,18},{18,26},{... | collective-permute-start | bytes 1032200 | tf_op jit(solution)/shard_map/ppermute | solution.py:18
  10.8 2.1 %collective-permute-start.1 = (bf16[4,28,1,12,128]{4,1,3,0,2:T(8,128)(2,1)S(1)}, bf16[4,28,1,12,128]{4,1,3,0,2:T(8,128)(2,1)S(1)}, u32[]{:S(2)}, u32[]{:S(2)}) collective-permute-start(bf16[4,28,1,12,128]{4,1,3,0,2:T(8,128)(2,1)S(1)} %bitcast.1361), channel_id=1, source_target_pairs={{8,0},{16,8},{24,16},{9,1},{17,9},{25,17},{10,2},{18,10},{26,18},{... | collective-permute-start | bytes 1032200 | tf_op jit(solution)/shard_map/ppermute | solution.py:19
  14.8 0.8 collective-permute-done
  15.5 4.4 %collective-permute-done.1 = bf16[4,28,1,12,128]{4,1,3,0,2:T(8,128)(2,1)S(1)} collective-permute-done((bf16[4,28,1,12,128]{4,1,3,0,2:T(8,128)(2,1)S(1)}, bf16[4,28,1,12,128]{4,1,3,0,2:T(8,128)(2,1)S(1)}, u32[]{:S(2)}, u32[]{:S(2)}) %collective-permute-start.1) | collective-permute-done | bytes 344096 | tf_op jit(solution)/shard_map/ppermute | solution.py:19
  19.9 1.7 %select_maximum_fusion.2 = bf16[4,28,3,14,130]{4,1,3,0,2:T(8,128)(2,1)S(1)} fusion(bf16[4,28,1,12,128]{4,1,3,0,2:T(8,128)(2,1)S(1)} %collective-permute-done.1, bf16[4,28,1,12,128]{4,1,3,0,2:T(8,128)(2,1)S(1)} %bitcast.1362, bf16[4,28,1,12,128]{4,1,3,0,2:T(8,128)(2,1)S(1)} %collective-permute-done), kind=kLoop, calls=%fused_computation.37 | loop fusion | flops 11618880 | bytes 2255232 | tf_op jit(solution)/shard_map/concatenate | solution.py:20
  27.9 0.7 fusion.69
  30.4 1.9 %collective-permute-start.2 = (bf16[4,56,1,12,128]{4,1,3,0,2:T(8,128)(2,1)S(1)}, bf16[4,56,1,12,128]{4,1,3,0,2:T(8,128)(2,1)S(1)}, u32[]{:S(2)}, u32[]{:S(2)}) collective-permute-start(bf16[4,56,1,12,128]{4,1,3,0,2:T(8,128)(2,1)S(1)} %pad_maximum_fusion), channel_id=1, source_target_pairs={{0,8},{8,16},{16,24},{1,9},{9,17},{17,25},{2,10},{10,18},{18,26},{... | collective-permute-start | bytes 2064392 | tf_op jit(solution)/shard_map/ppermute | solution.py:18
  32.3 2.7 %collective-permute-start.3 = (bf16[4,56,1,12,128]{4,1,3,0,2:T(8,128)(2,1)S(1)}, bf16[4,56,1,12,128]{4,1,3,0,2:T(8,128)(2,1)S(1)}, u32[]{:S(2)}, u32[]{:S(2)}) collective-permute-start(bf16[4,56,1,12,128]{4,1,3,0,2:T(8,128)(2,1)S(1)} %pad_maximum_fusion), channel_id=1, source_target_pairs={{8,0},{16,8},{24,16},{9,1},{17,9},{25,17},{10,2},{18,10},{26,18},{... | collective-permute-start | bytes 2064392 | tf_op jit(solution)/shard_map/ppermute | solution.py:19
  35.4 4.7 %collective-permute-done.2 = bf16[4,56,1,12,128]{4,1,3,0,2:T(8,128)(2,1)S(1)} collective-permute-done((bf16[4,56,1,12,128]{4,1,3,0,2:T(8,128)(2,1)S(1)}, bf16[4,56,1,12,128]{4,1,3,0,2:T(8,128)(2,1)S(1)}, u32[]{:S(2)}, u32[]{:S(2)}) %collective-permute-start.2) | collective-permute-done | bytes 688160 | tf_op jit(solution)/shard_map/ppermute | solution.py:18
  40.2 4.4 %collective-permute-done.3 = bf16[4,56,1,12,128]{4,1,3,0,2:T(8,128)(2,1)S(1)} collective-permute-done((bf16[4,56,1,12,128]{4,1,3,0,2:T(8,128)(2,1)S(1)}, bf16[4,56,1,12,128]{4,1,3,0,2:T(8,128)(2,1)S(1)}, u32[]{:S(2)}, u32[]{:S(2)}) %collective-permute-start.3) | collective-permute-done | bytes 688160 | tf_op jit(solution)/shard_map/ppermute | solution.py:19
  44.6 4.0 %fusion.19 = bf16[4,56,3,14,130]{4,1,3,0,2:T(8,128)(2,1)S(1)} fusion(bf16[4,56,1,12,128]{4,1,3,0,2:T(8,128)(2,1)S(1)} %collective-permute-done.3, bf16[4,56,1,12,128]{4,1,3,0,2:T(8,128)(2,1)S(1)} %collective-permute-done.2, bf16[4,28,1,12,128]{4,1,3,0,2:T(8,128)(2,1)S(1)} %copy.144, bf16[4,28,1,12,128]{4,1,3,0,2:T(8,128)(2,1)S(1)} %fusion.115), kind=kLoop, calls=%fused_computation.34 | loop fusion | flops 28129920 | bytes 4510464 | tf_op jit(solution)/shard_map/concatenate | solution.py:20
  56.0 0.8 fusion.38
  58.4 1.9 %collective-permute-start.4 = (bf16[4,56,1,12,128]{4,1,3,0,2:T(8,128)(2,1)S(1)}, bf16[4,56,1,12,128]{4,1,3,0,2:T(8,128)(2,1)S(1)}, u32[]{:S(2)}, u32[]{:S(2)}) collective-permute-start(bf16[4,56,1,12,128]{4,1,3,0,2:T(8,128)(2,1)S(1)} %pad_maximum_fusion.1), channel_id=1, source_target_pairs={{0,8},{8,16},{16,24},{1,9},{9,17},{17,25},{2,10},{10,18},{18,26},{... | collective-permute-start | bytes 2064392 | tf_op jit(solution)/shard_map/ppermute | solution.py:18
  60.3 2.7 %collective-permute-start.5 = (bf16[4,56,1,12,128]{4,1,3,0,2:T(8,128)(2,1)S(1)}, bf16[4,56,1,12,128]{4,1,3,0,2:T(8,128)(2,1)S(1)}, u32[]{:S(2)}, u32[]{:S(2)}) collective-permute-start(bf16[4,56,1,12,128]{4,1,3,0,2:T(8,128)(2,1)S(1)} %pad_maximum_fusion.1), channel_id=1, source_target_pairs={{8,0},{16,8},{24,16},{9,1},{17,9},{25,17},{10,2},{18,10},{26,18},{... | collective-permute-start | bytes 2064392 | tf_op jit(solution)/shard_map/ppermute | solution.py:19
  63.4 4.7 %collective-permute-done.4 = bf16[4,56,1,12,128]{4,1,3,0,2:T(8,128)(2,1)S(1)} collective-permute-done((bf16[4,56,1,12,128]{4,1,3,0,2:T(8,128)(2,1)S(1)}, bf16[4,56,1,12,128]{4,1,3,0,2:T(8,128)(2,1)S(1)}, u32[]{:S(2)}, u32[]{:S(2)}) %collective-permute-start.4) | collective-permute-done | bytes 688160 | tf_op jit(solution)/shard_map/ppermute | solution.py:18
  68.2 4.4 %collective-permute-done.5 = bf16[4,56,1,12,128]{4,1,3,0,2:T(8,128)(2,1)S(1)} collective-permute-done((bf16[4,56,1,12,128]{4,1,3,0,2:T(8,128)(2,1)S(1)}, bf16[4,56,1,12,128]{4,1,3,0,2:T(8,128)(2,1)S(1)}, u32[]{:S(2)}, u32[]{:S(2)}) %collective-permute-start.5) | collective-permute-done | bytes 688160 | tf_op jit(solution)/shard_map/ppermute | solution.py:19
  72.6 4.0 %select_maximum_fusion = bf16[4,56,3,14,130]{4,1,3,0,2:T(8,128)(2,1)S(1)} fusion(bf16[4,56,1,12,128]{4,1,3,0,2:T(8,128)(2,1)S(1)} %collective-permute-done.5, bf16[4,56,1,12,128]{4,1,3,0,2:T(8,128)(2,1)S(1)} %collective-permute-done.4, bf16[4,28,1,12,128]{4,1,3,0,2:T(8,128)(2,1)S(1)} %bitcast.1364, bf16[4,28,1,12,128]{4,1,3,0,2:T(8,128)(2,1)S(1)} %fusion.117), kind=kLoop, calls=%fused_computation.19 | loop fusion | flops 28129920 | bytes 4510464 | tf_op jit(solution)/shard_map/concatenate | solution.py:20
  81.8 1.2 convolution_bitcast_fusion.2
  83.0 1.3 convolution_bitcast_fusion.3
  84.2 1.2 convolution_bitcast_fusion.5
  85.4 1.3 convolution_bitcast_fusion.6
  86.7 1.3 convolution_bitcast_fusion.7
  88.0 1.2 convolution_bitcast_fusion.8
  89.4 0.8 fusion.52
  90.3 1.3 fusion.112
  91.6 1.1 convolution_bitcast_fusion.4
  92.7 4.0 %fusion.128 = f32[4,3,1,12,128]{4,1,3,0,2:T(4,128)S(1)} fusion(f32[4,28,1,12,128]{4,1,3,0,2:T(8,128)S(1)} %convolution_bitcast_fusion, f32[4,28,1,12,128]{4,1,3,0,2:T(8,128)S(1)} %convolution_bitcast_fusion.1, f32[4,28,1,12,128]{4,1,3,0,2:T(8,128)} %convolution_bitcast_fusion.2, f32[4,28,1,12,128]{4,1,3,0,2:T(8,128)} %convolution_bitcast_fusion.3, ...), kind=kOutput, calls=%fused_computation.203 | convolution fusion | flops 22628352 | bytes 8644608 | tf_op jit(solution)/shard_map/oc,mczay->mozay/dot_general | solution.py:119
  96.8 32.2 %while.1 = (s32[]{:T(128)}, f32[4,3,1,16,128]{4,3,2,1,0:T(8,128)S(1)}, s32[4,5]{1,0:T(4,128)S(1)}, f32[4,3,1,12,128]{4,1,3,0,2:T(4,128)S(1)}, s32[]{:T(128)}, /*index=5*/s32[5]{0:T(128)S(1)}, s32[]{:T(128)}) while((s32[]{:T(128)}, f32[4,3,1,16,128]{4,3,2,1,0:T(8,128)S(1)}, s32[4,5]{1,0:T(4,128)S(1)}, f32[4,3,1,12,128]{4,1,3,0,2:T(4,128)S(1)}, ...), condition=%wide.while_cond, body=%wide.while_body.sunk | while | flops 4629 | bytes 129283 | solution.py:127
  97.5 3.3 %concatenate.35 = s32[5]{0:T(128)S(1)} concatenate(s32[1]{0:T(128)} %bitcast.1355, s32[1]{0:T(128)} %bitcast.1356, s32[1]{0:T(128)} %bitcast.1357, s32[1]{0:T(128)} %bitcast.1358, s32[1]{0:T(128)} %bitcast.1359), dimensions={0} | concatenate | bytes 40 | tf_op jit(solution)/shard_map/vmap(vmap())/scatter
  100.7 0.7 and_reduce_fusion.2
  101.4 1.9 %copy_select_fusion.2 = f32[1,3,1,12,128]{4,3,2,1,0:T(8,128)S(1)} fusion(f32[1,3,1,12,128]{4,1,3,0,2:T(4,128)S(1)} %constant_dynamic-slice_fusion.7, f32[4,3,1,16,128]{4,3,2,1,0:T(8,128)S(1)} %get-tuple-element.91, s32[]{:T(128)} %bitcast.1353, s32[]{:T(128)} %bitcast.1354, pred[]{:T(512)} %and_reduce_fusion.2), kind=kLoop, calls=%fused_computation.1.clone.1 | loop fusion | flops 4608 | bytes 55305 | tf_op jit(solution)/shard_map/vmap(vmap())/scatter
  103.4 1.4 dynamic-update-slice.3
  105.5 3.3 %concatenate.35 = s32[5]{0:T(128)S(1)} concatenate(s32[1]{0:T(128)} %bitcast.1355, s32[1]{0:T(128)} %bitcast.1356, s32[1]{0:T(128)} %bitcast.1357, s32[1]{0:T(128)} %bitcast.1358, s32[1]{0:T(128)} %bitcast.1359), dimensions={0} | concatenate | bytes 40 | tf_op jit(solution)/shard_map/vmap(vmap())/scatter
  108.8 0.7 and_reduce_fusion.2
  109.5 1.9 %copy_select_fusion.2 = f32[1,3,1,12,128]{4,3,2,1,0:T(8,128)S(1)} fusion(f32[1,3,1,12,128]{4,1,3,0,2:T(4,128)S(1)} %constant_dynamic-slice_fusion.7, f32[4,3,1,16,128]{4,3,2,1,0:T(8,128)S(1)} %get-tuple-element.91, s32[]{:T(128)} %bitcast.1353, s32[]{:T(128)} %bitcast.1354, pred[]{:T(512)} %and_reduce_fusion.2), kind=kLoop, calls=%fused_computation.1.clone.1 | loop fusion | flops 4608 | bytes 55305 | tf_op jit(solution)/shard_map/vmap(vmap())/scatter
  111.4 1.4 dynamic-update-slice.3
  113.6 3.3 %concatenate.35 = s32[5]{0:T(128)S(1)} concatenate(s32[1]{0:T(128)} %bitcast.1355, s32[1]{0:T(128)} %bitcast.1356, s32[1]{0:T(128)} %bitcast.1357, s32[1]{0:T(128)} %bitcast.1358, s32[1]{0:T(128)} %bitcast.1359), dimensions={0} | concatenate | bytes 40 | tf_op jit(solution)/shard_map/vmap(vmap())/scatter
  117.6 1.9 %copy_select_fusion.2 = f32[1,3,1,12,128]{4,3,2,1,0:T(8,128)S(1)} fusion(f32[1,3,1,12,128]{4,1,3,0,2:T(4,128)S(1)} %constant_dynamic-slice_fusion.7, f32[4,3,1,16,128]{4,3,2,1,0:T(8,128)S(1)} %get-tuple-element.91, s32[]{:T(128)} %bitcast.1353, s32[]{:T(128)} %bitcast.1354, pred[]{:T(512)} %and_reduce_fusion.2), kind=kLoop, calls=%fused_computation.1.clone.1 | loop fusion | flops 4608 | bytes 55305 | tf_op jit(solution)/shard_map/vmap(vmap())/scatter
  119.5 1.4 dynamic-update-slice.3
  121.6 3.3 %concatenate.35 = s32[5]{0:T(128)S(1)} concatenate(s32[1]{0:T(128)} %bitcast.1355, s32[1]{0:T(128)} %bitcast.1356, s32[1]{0:T(128)} %bitcast.1357, s32[1]{0:T(128)} %bitcast.1358, s32[1]{0:T(128)} %bitcast.1359), dimensions={0} | concatenate | bytes 40 | tf_op jit(solution)/shard_map/vmap(vmap())/scatter
  125.6 1.9 %copy_select_fusion.2 = f32[1,3,1,12,128]{4,3,2,1,0:T(8,128)S(1)} fusion(f32[1,3,1,12,128]{4,1,3,0,2:T(4,128)S(1)} %constant_dynamic-slice_fusion.7, f32[4,3,1,16,128]{4,3,2,1,0:T(8,128)S(1)} %get-tuple-element.91, s32[]{:T(128)} %bitcast.1353, s32[]{:T(128)} %bitcast.1354, pred[]{:T(512)} %and_reduce_fusion.2), kind=kLoop, calls=%fused_computation.1.clone.1 | loop fusion | flops 4608 | bytes 55305 | tf_op jit(solution)/shard_map/vmap(vmap())/scatter
  127.6 1.4 dynamic-update-slice.3
  129.8 0.7 copy.46
  130.6 5.6 %all-to-all-start = ((f32[8,4,3,1,4,128]{5,1,4,2,3,0:T(4,128)}), f32[8,4,3,1,4,128]{5,1,4,2,3,0:T(4,128)S(1)}, u32[]{:S(2)}, u32[]{:S(2)}) async-start(f32[8,4,3,1,4,128]{5,1,4,2,3,0:T(4,128)} %copy.46), calls=%async_computation | async-start | bytes 393216 | tf_op jit(solution)/shard_map/all_to_all | solution.py:136
  136.2 6.6 %all-to-all-done = f32[8,4,3,1,4,128]{5,1,4,2,3,0:T(4,128)S(1)} async-done(((f32[8,4,3,1,4,128]{5,1,4,2,3,0:T(4,128)}), f32[8,4,3,1,4,128]{5,1,4,2,3,0:T(4,128)S(1)}, u32[]{:S(2)}, u32[]{:S(2)}) %all-to-all-start) | async-done | bytes 196640 | tf_op jit(solution)/shard_map/all_to_all | solution.py:136
  (160 shorter events, 33.7 us)
Async XLA Ops:
  0.0 1.3 copy-start
  0.0 4.1 %copy-start.7 = (bf16[9,28,28]{2,1,0:T(8,128)(2,1)S(1)}, bf16[9,28,28]{2,1,0:T(8,128)(2,1)}, u32[]{:S(2)}) copy-start(bf16[9,28,28]{2,1,0:T(8,128)(2,1)} %param.16) | copy-start | bytes 42340
  4.5 1.5 %copy-start.9 = (f32[28]{0:T(128)S(1)}, f32[28]{0:T(128)}, u32[]{:S(2)}) copy-start(f32[28]{0:T(128)} %param.17) | copy-start | bytes 340
  4.8 8.2 %copy-start.3 = (bf16[4,28,4,12,128]{4,2,3,1,0:T(4,128)(2,1)S(1)}, bf16[4,28,4,12,128]{4,2,3,1,0:T(4,128)(2,1)}, u32[]{:S(2)}) copy-start(bf16[4,28,4,12,128]{4,2,3,1,0:T(4,128)(2,1)} %param.15) | copy-start | bytes 4128772
  5.1 8.8 %copy-start.16 = (s32[32]{0:T(128)S(1)}, s32[32]{0:T(128)}, u32[]{:S(2)}) copy-start(s32[32]{0:T(128)} %param.27) | copy-start | bytes 388
  5.1 9.1 %copy-start.13 = (s32[32]{0:T(128)S(1)}, s32[32]{0:T(128)}, u32[]{:S(2)}) copy-start(s32[32]{0:T(128)} %param.26) | copy-start | bytes 388
  5.1 9.4 %copy-start.4 = (bf16[27,28,28]{2,1,0:T(8,128)(2,1)S(1)}, bf16[27,28,28]{2,1,0:T(8,128)(2,1)}, u32[]{:S(2)}) copy-start(bf16[27,28,28]{2,1,0:T(8,128)(2,1)} %param.18) | copy-start | bytes 127012
  6.3 9.2 %collective-permute-start = (bf16[4,28,1,12,128]{4,1,3,0,2:T(8,128)(2,1)S(1)}, bf16[4,28,1,12,128]{4,1,3,0,2:T(8,128)(2,1)S(1)}, u32[]{:S(2)}, u32[]{:S(2)}) collective-permute-start(bf16[4,28,1,12,128]{4,1,3,0,2:T(8,128)(2,1)S(1)} %bitcast.1360), channel_id=1, source_target_pairs={{0,8},{8,16},{16,24},{1,9},{9,17},{17,25},{2,10},{10,18},{18,26},{... | collective-permute-start | bytes 1032200 | tf_op jit(solution)/shard_map/ppermute | solution.py:18
  10.8 9.1 %collective-permute-start.1 = (bf16[4,28,1,12,128]{4,1,3,0,2:T(8,128)(2,1)S(1)}, bf16[4,28,1,12,128]{4,1,3,0,2:T(8,128)(2,1)S(1)}, u32[]{:S(2)}, u32[]{:S(2)}) collective-permute-start(bf16[4,28,1,12,128]{4,1,3,0,2:T(8,128)(2,1)S(1)} %bitcast.1361), channel_id=1, source_target_pairs={{8,0},{16,8},{24,16},{9,1},{17,9},{25,17},{10,2},{18,10},{26,18},{... | collective-permute-start | bytes 1032200 | tf_op jit(solution)/shard_map/ppermute | solution.py:19
  28.6 0.9 copy-start.10
  29.5 5.5 %copy-start.14 = (s32[4]{0:T(128)S(1)}, s32[4]{0:T(128)}, u32[]{:S(2)}) copy-start(s32[4]{0:T(128)} %constant.95.clone.1) | copy-start | bytes 52
  29.5 5.7 %copy-start.6 = (bf16[27,28,56]{2,1,0:T(8,128)(2,1)S(1)}, bf16[27,28,56]{2,1,0:T(8,128)(2,1)}, u32[]{:S(2)}) copy-start(bf16[27,28,56]{2,1,0:T(8,128)(2,1)} %param.20) | copy-start | bytes 254020
  30.4 9.8 %collective-permute-start.2 = (bf16[4,56,1,12,128]{4,1,3,0,2:T(8,128)(2,1)S(1)}, bf16[4,56,1,12,128]{4,1,3,0,2:T(8,128)(2,1)S(1)}, u32[]{:S(2)}, u32[]{:S(2)}) collective-permute-start(bf16[4,56,1,12,128]{4,1,3,0,2:T(8,128)(2,1)S(1)} %pad_maximum_fusion), channel_id=1, source_target_pairs={{0,8},{8,16},{16,24},{1,9},{9,17},{17,25},{2,10},{10,18},{18,26},{... | collective-permute-start | bytes 2064392 | tf_op jit(solution)/shard_map/ppermute | solution.py:18
  32.3 12.3 %collective-permute-start.3 = (bf16[4,56,1,12,128]{4,1,3,0,2:T(8,128)(2,1)S(1)}, bf16[4,56,1,12,128]{4,1,3,0,2:T(8,128)(2,1)S(1)}, u32[]{:S(2)}, u32[]{:S(2)}) collective-permute-start(bf16[4,56,1,12,128]{4,1,3,0,2:T(8,128)(2,1)S(1)} %pad_maximum_fusion), channel_id=1, source_target_pairs={{8,0},{16,8},{24,16},{9,1},{17,9},{25,17},{10,2},{18,10},{26,18},{... | collective-permute-start | bytes 2064392 | tf_op jit(solution)/shard_map/ppermute | solution.py:19
  56.8 0.7 copy-start.15
  57.5 5.7 %copy-start.5 = (bf16[27,28,56]{2,1,0:T(8,128)(2,1)S(1)}, bf16[27,28,56]{2,1,0:T(8,128)(2,1)}, u32[]{:S(2)}) copy-start(bf16[27,28,56]{2,1,0:T(8,128)(2,1)} %param.22) | copy-start | bytes 254020
  58.4 9.8 %collective-permute-start.4 = (bf16[4,56,1,12,128]{4,1,3,0,2:T(8,128)(2,1)S(1)}, bf16[4,56,1,12,128]{4,1,3,0,2:T(8,128)(2,1)S(1)}, u32[]{:S(2)}, u32[]{:S(2)}) collective-permute-start(bf16[4,56,1,12,128]{4,1,3,0,2:T(8,128)(2,1)S(1)} %pad_maximum_fusion.1), channel_id=1, source_target_pairs={{0,8},{8,16},{16,24},{1,9},{9,17},{17,25},{2,10},{10,18},{18,26},{... | collective-permute-start | bytes 2064392 | tf_op jit(solution)/shard_map/ppermute | solution.py:18
  60.3 12.3 %collective-permute-start.5 = (bf16[4,56,1,12,128]{4,1,3,0,2:T(8,128)(2,1)S(1)}, bf16[4,56,1,12,128]{4,1,3,0,2:T(8,128)(2,1)S(1)}, u32[]{:S(2)}, u32[]{:S(2)}) collective-permute-start(bf16[4,56,1,12,128]{4,1,3,0,2:T(8,128)(2,1)S(1)} %pad_maximum_fusion.1), channel_id=1, source_target_pairs={{8,0},{16,8},{24,16},{9,1},{17,9},{25,17},{10,2},{18,10},{26,18},{... | collective-permute-start | bytes 2064392 | tf_op jit(solution)/shard_map/ppermute | solution.py:19
  76.5 13.7 %copy-start.2 = (bf16[4,56,3,14,130]{4,1,3,0,2:T(8,128)(2,1)}, bf16[4,56,3,14,130]{4,1,3,0,2:T(8,128)(2,1)S(1)}, u32[]{:S(2)}) copy-start(bf16[4,56,3,14,130]{4,1,3,0,2:T(8,128)(2,1)S(1)} %select_maximum_fusion) | copy-start | bytes 7338244
  90.3 2.5 %copy-start.8 = (bf16[3,28]{1,0:T(4,128)(2,1)S(1)}, bf16[3,28]{1,0:T(4,128)(2,1)}, u32[]{:S(2)}) copy-start(bf16[3,28]{1,0:T(4,128)(2,1)} %param.24) | copy-start | bytes 508
  90.3 2.5 %copy-start.11 = (f32[28]{0:T(128)S(1)}, f32[28]{0:T(128)}, u32[]{:S(2)}) copy-start(f32[28]{0:T(128)} %param.23) | copy-start | bytes 340
  90.3 2.5 %copy-start.12 = (f32[3]{0:T(128)S(1)}, f32[3]{0:T(128)}, u32[]{:S(2)}) copy-start(f32[3]{0:T(128)} %param.25) | copy-start | bytes 40
  91.6 5.2 %copy-start.17 = (s32[5]{0:T(128)S(1)}, s32[5]{0:T(128)}, u32[]{:S(2)}) copy-start(s32[5]{0:T(128)} %constant.505) | copy-start | bytes 64
  91.6 52.2 %copy-start.1 = (bf16[4,28,4,12,128]{4,2,3,1,0:T(4,128)(2,1)S(1)}, bf16[4,28,4,12,128]{4,2,3,1,0:T(4,128)(2,1)}, u32[]{:S(2)}) copy-start(bf16[4,28,4,12,128]{4,2,3,1,0:T(4,128)(2,1)} %param.14) | copy-start | bytes 4128772
  130.6 12.2 %all-to-all-start = ((f32[8,4,3,1,4,128]{5,1,4,2,3,0:T(4,128)}), f32[8,4,3,1,4,128]{5,1,4,2,3,0:T(4,128)S(1)}, u32[]{:S(2)}, u32[]{:S(2)}) async-start(f32[8,4,3,1,4,128]{5,1,4,2,3,0:T(4,128)} %copy.46), calls=%async_computation | async-start | bytes 393216 | tf_op jit(solution)/shard_map/all_to_all | solution.py:136
where the time goes:
time: 145 us; the launch traced here: 144 us
  matrix products  42.9 us (30%)
  waiting for transfers between devices  30 us (21%)
  local copies, waits for them, and re-layouts  27.1 us (19%)
  starting transfers between devices  21.4 us (15%)
  other arithmetic  21.4 us (15%)
    dot_general x80, matrix products, convolve_inner(): jnp.einsum('oc,czay->ozay', kernel[depth_shift * 9 + row_shift * 3 + col_...  34.7 us
    scatter x20, local copies, waits for them, and re-layouts  21.5 us
    ppermute x3, waiting for transfers between devices, extended(): after = lax.ppermute(first, axis, down)  13.2 us
    scatter x8, other arithmetic  10.6 us
    ppermute x3, waiting for transfers between devices, extended(): before = lax.ppermute(last, axis, up)  10.2 us
    concatenate x3, other arithmetic, extended(): array = jnp.concatenate([before, array, after], axis=dim)  9.63 us
    ppermute x3, starting transfers between devices, extended(): before = lax.ppermute(last, axis, up)  8.35 us
    ppermute x3, starting transfers between devices, extended(): after = lax.ppermute(first, axis, down)  7.47 us
  transfers between devices with their start and end apart: 7, of which 7 were waited for; matrix products, arithmetic and copies ran while one was open for 2% of the time, Pallas kernels for 0%

commit v1 on v0

v1 whole, which is shorter than its diff:
```python
import functools
import math

import jax
import jax.numpy as jnp
import numpy as np
from jax import lax
from jax.experimental import pallas as pl
from jax.experimental.pallas import tpu as pltpu
from jax.sharding import PartitionSpec as P

CW = 4
CH_DEV = 8
KMAX = 4
LANES = 128
SLOT = 32
GROUP = 4
BF = jnp.bfloat16
F32 = jnp.float32


def bump(count):
    place = (np.arange(count).astype(np.float32) + np.float32(0.5)) / np.float32(count)
    return (np.sin(np.float32(np.pi) * place) ** 2).astype(np.float32)


def lane_index(rows):
    return lax.broadcasted_iota(jnp.int32, (rows, LANES), 1)


def put_shifted(act, row, value):
    rows = value.shape[0]
    lane = lane_index(rows)
    act[1, pl.ds(row, rows), :] = value.astype(BF)
    act[0, pl.ds(row, rows), :] = jnp.where(lane == 0, 0.0, pltpu.roll(value, 1, 1)).astype(BF)
    act[2, pl.ds(row, rows), :] = jnp.where(
        lane == LANES - 1, 0.0, pltpu.roll(value, LANES - 1, 1)
    ).astype(BF)


def build_taps(weight, low, chans, strip, big, depth):
    lane = lane_index(SLOT)
    for dy in range(3):
        for da in range(3):
            k = dy * 3 + da
            for dz in range(3):
                strip[k, 0:chans, dz * SLOT : dz * SLOT + chans] = weight[
                    9 * dz + 3 * da + dy, :, low : low + chans
                ].astype(F32)
            base = strip[k]
            for z in range(depth):
                shift = ((z - 1) * SLOT) % LANES
                moved = pltpu.roll(base, shift, 1) if shift else base
                if z == 0:
                    moved = jnp.where(lane < LANES - SLOT, moved, 0.0)
                if z == depth - 1:
                    moved = jnp.where(lane >= SLOT, moved, 0.0)
                big[z * SLOT : (z + 1) * SLOT, k * LANES : (k + 1) * LANES] = moved.astype(BF)


def column(row_ref, pad, rows, pick):
    pad[...] = jnp.zeros(pad.shape, F32)
    pad[0:1, 0 : row_ref.shape[1]] = row_ref[...]
    spread = jnp.broadcast_to(pad[0:1, :], (rows, LANES))
    want = pick(lax.broadcasted_iota(jnp.int32, (rows, LANES), 0))
    return jnp.sum(jnp.where(lane_index(rows) == want, spread, 0.0), axis=1, keepdims=True)


def unet_kernel(
    owners,
    first_block,
    offset,
    features,
    deep,
    w1,
    w2,
    w3,
    w4,
    b1,
    b2,
    b3,
    b4,
    hw,
    hb,
    wy,
    out,
    feat_v,
    deep_v,
    w1_v,
    w2_v,
    w3_v,
    w4_v,
    cells,
    xf,
    x1,
    x2,
    xd,
    x3,
    m1,
    m2,
    m3s,
    m3d,
    m4t,
    m4f,
    strip,
    pad,
    head,
    sems,
):
    chans, depth, along = feat_v.shape[0], feat_v.shape[1], feat_v.shape[2]
    plane = depth * SLOT
    me = lax.axis_index("segment")
    patch = lax.axis_index("patch") * features.shape[0] + me

    copies = [
        pltpu.make_async_copy(src, dst, sems.at[i])
        for i, (src, dst) in enumerate(
            [
                (features.at[me], feat_v),
                (w1, w1_v),
                (w2, w2_v),
                (deep.at[me], deep_v),
                (w3, w3_v),
                (w4, w4_v),
            ]
        )
    ]
    for c in copies:
        c.start()

    for act in (x1, x2, xd, x3):
        for dy in range(3):
            act[dy, 0:plane, :] = jnp.zeros((plane, LANES), BF)
            act[dy, (along + 1) * plane : (along + 2) * plane, :] = jnp.zeros((plane, LANES), BF)
    high = (along + 2) * SLOT
    for dy in range(3):
        for z in range(depth):
            xf[dy, z * high : z * high + SLOT, :] = jnp.zeros((SLOT, LANES), BF)
            xf[dy, (z + 1) * high - SLOT : (z + 1) * high, :] = jnp.zeros((SLOT, LANES), BF)
    m1[...] = jnp.zeros(m1.shape, F32)
    strip[...] = jnp.zeros(strip.shape, F32)
    head[...] = jnp.zeros(head.shape, F32)
    out[...] = jnp.zeros(out.shape, F32)
    rows16 = 16
    cells[chans * depth * rows16 :, :] = jnp.zeros(
        (cells.shape[0] - chans * depth * rows16, LANES), F32
    )

    def spread_cells(source):
        for c in range(chans):
            for z in range(depth):
                cells[pl.ds((c * depth + z) * rows16, along), :] = source[c, z].astype(F32)

    def gathered(z, a):
        return cells[pl.ds(z * rows16 + a, SLOT, stride=depth * rows16), :]

    def own(r):
        return r

    copies[0].wait()
    spread_cells(feat_v)
    for z in range(depth):
        for a in range(along):
            put_shifted(xf, z * high + (a + 1) * SLOT, gathered(z, a))

    copies[1].wait()
    span = (GROUP + 2) * SLOT
    for dy in range(3):
        for da in range(3):
            tap = w1_v[da * 3 + dy].astype(F32)
            for a in range(GROUP):
                lo = dy * span + (a + da) * SLOT
                m1[a * SLOT : a * SLOT + chans, lo : lo + chans] = tap
    m1_b = m1[...].astype(BF)

    def bias_rows(ref, copies_of):
        col = column(ref, pad, SLOT, own)
        tile = jnp.broadcast_to(col, (SLOT, LANES))
        return jnp.concatenate([tile] * copies_of, axis=0)

    bias = bias_rows(b1, GROUP)
    for z in range(depth):
        for pair in range(0, along // GROUP):
            rhs = jnp.concatenate(
                [xf[dy, pl.ds(z * high + pair * GROUP * SLOT, span), :] for dy in range(3)], axis=0
            )
            got = jnp.dot(m1_b, rhs, preferred_element_type=F32)
            got = jnp.maximum(got + bias, 0.0)
            for a in range(GROUP):
                put_shifted(
                    x1,
                    (1 + pair * GROUP + a) * plane + z * SLOT,
                    got[a * SLOT : (a + 1) * SLOT],
                )

    def window_of(act, a):
        return jnp.concatenate([act[dy, pl.ds(a * plane, 3 * plane), :] for dy in range(3)], axis=0)

    def conv(mats, acts, bias, a):
        matrix = jnp.concatenate([m[...] for m in mats], axis=1) if len(mats) > 1 else mats[0][...]
        cols = []
        for b in (a, a + 1):
            parts = [window_of(x, b) for x in acts]
            cols.append(jnp.concatenate(parts, axis=0) if len(parts) > 1 else parts[0])
        got = jnp.dot(matrix, jnp.concatenate(cols, axis=1), preferred_element_type=F32)
        wide = jnp.concatenate([bias, bias], axis=1)
        return jnp.maximum(got + wide, 0.0)

    def layer(mats, acts, bias, result):
        for a in range(0, along, 2):
            got = conv(mats, acts, bias, a)
            for h in range(2):
                put_shifted(result, (1 + a + h) * plane, got[:, h * LANES : (h + 1) * LANES])

    copies[2].wait()
    build_taps(w2_v, 0, chans, strip.at[0], m2, depth)
    layer([m2], [x1], bias_rows(b2, depth), x2)

    copies[3].wait()
    spread_cells(deep_v)
    for z in range(depth):
        for a in range(along):
            put_shifted(xd, (a + 1) * plane + z * SLOT, gathered(z, a))
    copies[4].wait()
    build_taps(w3_v, 0, chans, strip.at[1], m3s, depth)
    build_taps(w3_v, chans, chans, strip.at[2], m3d, depth)
    layer([m3s, m3d], [x2, xd], bias_rows(b3, depth), x3)

    copies[5].wait()
    build_taps(w4_v, 0, chans, strip.at[3], m4t, depth)
    build_taps(w4_v, chans, chans, strip.at[4], m4f, depth)
    bias = bias_rows(b4, depth)
    kinds = hw.shape[0]
    tap = hw[...].astype(F32)
    for z in range(depth):
        head[z * 4 : z * 4 + kinds, z * SLOT : z * SLOT + chans] = tap
    head_b = head[...].astype(BF)
    head_bias = column(hb, pad, 4 * depth, lambda r: r % 4)
    sz, sa = bump(depth), bump(along)
    row = lax.broadcasted_iota(jnp.int32, (4 * depth, LANES), 0)
    blend_z = jnp.full((4 * depth, LANES), float(sz[0]), F32)
    for z in range(1, depth):
        blend_z = jnp.where(row >= 4 * z, float(sz[z]), blend_z)
    across = jnp.broadcast_to(wy[...], (4 * depth, LANES))
    start = first_block[patch]
    move = offset[patch]
    for a in range(0, along, 2):
        fourth = conv([m4t, m4f], [x3, x1], bias, a).astype(BF)
        logits = jnp.dot(head_b, fourth, preferred_element_type=F32) + head_bias
        value = jax.nn.sigmoid(logits)
        for h in range(2):
            part = value[:, h * LANES : (h + 1) * LANES] * (
                blend_z * float(sa[a + h]) * across
            )
            place = move + (a + h)
            owner = lax.rem(start + place // CW, owners)
            cell = lax.rem(place, CW)
            for z in range(depth):
                for kind in range(kinds):
                    r = z * 4 + kind
                    out[z * owners + owner, kind, pl.ds(cell, 1), :] = part[r : r + 1, :]


def blend_kernel(owners, segments, first_block, mine, out):
    owner = lax.axis_index("patch")
    out[...] = jnp.zeros(out.shape, F32)
    for src in range(mine.shape[0]):
        patch = (src % owners) * segments + src // owners
        first = first_block[patch]
        ahead = lax.rem(owner - first + owners * CH_DEV, owners)
        index = jnp.minimum((first + ahead) // owners, CH_DEV - 1)
        out[index] += mine[src]


def per_device(
    features,
    deep_path,
    weight_first,
    bias_first,
    weight_second,
    bias_second,
    weight_third,
    bias_third,
    weight_fourth,
    bias_fourth,
    head_weight,
    head_bias,
    block_first,
    block_offset,
):
    segments = lax.axis_size("segment")
    owners = lax.axis_size("patch")
    count, chans, depth, along, across = features.shape
    kinds = head_weight.shape[0]
    assert count == segments and depth == segments and across == LANES
    assert along % GROUP == 0 and chans <= SLOT and depth * SLOT == LANES
    plane = depth * SLOT
    vmem = pl.BlockSpec(memory_space=pltpu.VMEM)
    smem = pl.BlockSpec(memory_space=pltpu.SMEM)
    hbm = pl.BlockSpec(memory_space=pl.ANY)
    act = pltpu.VMEM((3, (along + 2) * plane, LANES), BF)
    taps = pltpu.VMEM((plane, 9 * LANES), BF)
    wy = jnp.asarray(bump(across)).reshape(1, across)
    slots = pl.pallas_call(
        functools.partial(unet_kernel, owners),
        out_shape=jax.ShapeDtypeStruct((segments * owners, kinds, CW, across), F32),
        in_specs=[smem, smem] + [hbm] * 6 + [vmem] * 7,
        out_specs=vmem,
        scratch_shapes=[
            pltpu.VMEM((chans, depth, along, across), BF),
            pltpu.VMEM((chans, depth, along, across), BF),
            pltpu.VMEM(weight_first.shape, BF),
            pltpu.VMEM(weight_second.shape, BF),
            pltpu.VMEM(weight_third.shape, BF),
            pltpu.VMEM(weight_fourth.shape, BF),
            pltpu.VMEM((SLOT * depth * 16, LANES), F32),
            pltpu.VMEM((3, depth * (along + 2) * SLOT, LANES), BF),
            act,
            act,
            act,
            act,
            pltpu.VMEM((GROUP * SLOT, 3 * (GROUP + 2) * SLOT), F32),
            taps,
            taps,
            taps,
            taps,
            taps,
            pltpu.VMEM((5, 9, SLOT, LANES), F32),
            pltpu.VMEM((8, LANES), F32),
            pltpu.VMEM((4 * depth, LANES), F32),
            pltpu.SemaphoreType.DMA((6,)),
        ],
        compiler_params=pltpu.CompilerParams(vmem_limit_bytes=48 * 2**20),
    )(
        block_first,
        block_offset,
        features,
        deep_path,
        weight_first,
        weight_second,
        weight_third,
        weight_fourth,
        bias_first.reshape(1, chans),
        bias_second.reshape(1, chans),
        bias_third.reshape(1, chans),
        bias_fourth.reshape(1, chans),
        head_weight,
        head_bias.reshape(1, kinds),
        wy,
    )
    mine = lax.all_to_all(slots, ("segment", "patch"), split_axis=0, concat_axis=0, tiled=True)
    blended = pl.pallas_call(
        functools.partial(blend_kernel, owners, segments),
        out_shape=jax.ShapeDtypeStruct((CH_DEV, kinds, CW, across), F32),
        in_specs=[smem, vmem],
        out_specs=vmem,
    )(block_first, mine)
    return blended.reshape(CH_DEV, 1, kinds, 1, CW, across)


def solution(mesh):
    rows = P("patch", None, None, None, None)
    return jax.shard_map(
        per_device,
        mesh=mesh,
        in_specs=(rows, rows) + (P(),) * 12,
        out_specs=P(None, "patch", None, "segment", None, None),
        check_vma=False,
    )
```

time: 145 us -> 30.9 us (0.21)
  the two profiles are of different devices: /device:TPU:1 before, /device:TPU:0 now
where the time goes in v1:
time: 30.9 us; the launch traced here: 30.7 us
  blocking collectives  15.8 us (51%)
  Pallas kernels  11.7 us (38%)
  local copies, waits for them, and re-layouts  3.1 us (10%)
    all_to_all x1, blocking collectives, per_device(): lax.all_to_all(slots, ('segment', 'patch'), split_axis=0, concat_axis=0,...  15.8 us
    pallas_call x1, Pallas kernels, per_device(): pl.pallas_call(functools.partial(unet_kernel, owners), out_shape=jax.Shap...  9.88 us
    unnamed x30, local copies, waits for them, and re-layouts  3.1 us
    pallas_call x1, Pallas kernels, per_device(): pl.pallas_call(functools.partial(blend_kernel, owners, segments), out_sha...  1.83 us

profile of v1, /device:TPU:0, one launch (start us, length us, event | category | flops | bytes accessed | tf_op | source)
XLA Modules:
  0.0 30.7 jit_solution(4982323954473422101)
XLA Ops:
  0.0 0.0 copy-start.13
  0.0 2.0 %copy.16.features = bf16[4,28,4,12,128]{4,3,2,1,0:T(8,128)(2,1)S(1)} copy(bf16[4,28,4,12,128]{4,2,3,1,0:T(4,128)(2,1)} %param.15) | data formatting | bytes 2752512 | tf_op args[0]
  2.0 0.0 copy-done.13
  2.0 0.0 copy-start
  2.0 0.0 copy-start.1
  2.0 0.0 copy-start.2
  2.0 0.0 copy-start.3
  2.0 0.0 copy-start.4
  2.0 0.0 copy-start.5
  2.1 0.0 copy-start.6
  2.1 0.0 copy-start.7
  2.1 0.0 copy-start.8
  2.1 0.0 copy-start.9
  2.1 0.0 copy-start.10
  2.1 0.0 copy-start.11
  2.1 0.0 copy-start.12
  2.1 0.5 %copy.17.deep = bf16[4,28,4,12,128]{4,3,2,1,0:T(8,128)(2,1)S(1)} copy(bf16[4,28,4,12,128]{4,2,3,1,0:T(4,128)(2,1)S(1)} %copy-done.13) | data formatting | bytes 2752512 | tf_op args[1]
  2.7 0.2 copy-done
  2.9 0.1 copy-done.1
  3.0 0.1 copy-done.2
  3.1 0.1 copy-done.3
  3.2 0.0 copy-done.4
  3.2 0.0 copy-done.5
  3.2 0.0 copy-done.6
  3.2 0.0 copy-done.7
  3.2 0.0 copy-done.8
  3.2 0.0 copy-done.9
  3.2 0.0 copy-done.10
  3.3 0.0 copy-done.11
  3.3 0.0 copy-done.12
  3.3 9.9 %shard_map.145 = f32[32,3,4,128]{3,2,1,0:T(4,128)S(1)} custom-call(s32[32]{0:T(128)S(1)} %copy-done.4, s32[32]{0:T(128)S(1)} %copy-done.6, bf16[4,28,4,12,128]{4,3,2,1,0:T(8,128)(2,1)S(1)} %copy.16.features, bf16[4,28,4,12,128]{4,3,2,1,0:T(8,128)(2,1)S(1)} %copy.17.deep, bf16[9,28,28]{2,1,0:T(8,128)(2,1)S(1)} %copy-done.3, bf16[27,28,28]{2,1,0:T(8,128)(2,1)S(1)} %copy-done, ...), custom_call_target="tpu_custom_call" | custom-call | tf_op jit(solution)/shard_map/pallas_call | solution.py:304
  13.2 15.8 %all_to_all.5.mine = f32[32,3,4,128]{3,2,1,0:T(4,128)} all-to-all(f32[32,3,4,128]{3,2,1,0:T(4,128)S(1)} %shard_map.145), channel_id=1, replica_groups=mesh['segment'=4,'patch'=8] {'segment','patch'}, dimensions={0} | all-to-all | bytes 393216 | tf_op jit(solution)/shard_map/all_to_all | solution.py:351
  28.9 1.8 %shard_map.146 = f32[8,3,4,128]{3,2,1,0:T(4,128)} custom-call(s32[32]{0:T(128)} %first_block.3, f32[32,3,4,128]{3,2,1,0:T(4,128)} %all_to_all.5.mine), custom_call_target="tpu_custom_call" | custom-call | tf_op jit(solution)/shard_map/pallas_call | solution.py:352
Async XLA Ops:
  0.0 2.0 %copy-start.13 = (bf16[4,28,4,12,128]{4,2,3,1,0:T(4,128)(2,1)S(1)}, bf16[4,28,4,12,128]{4,2,3,1,0:T(4,128)(2,1)}, u32[]{:S(2)}) copy-start(bf16[4,28,4,12,128]{4,2,3,1,0:T(4,128)(2,1)} %param.16) | copy-start | bytes 4128772
  2.0 0.9 %copy-start = (bf16[27,28,28]{2,1,0:T(8,128)(2,1)S(1)}, bf16[27,28,28]{2,1,0:T(8,128)(2,1)}, u32[]{:S(2)}) copy-start(bf16[27,28,28]{2,1,0:T(8,128)(2,1)} %w2.1) | copy-start | bytes 127012
  2.0 1.0 %copy-start.1 = (bf16[27,28,56]{2,1,0:T(8,128)(2,1)S(1)}, bf16[27,28,56]{2,1,0:T(8,128)(2,1)}, u32[]{:S(2)}) copy-start(bf16[27,28,56]{2,1,0:T(8,128)(2,1)} %w3.1) | copy-start | bytes 254020
  2.0 1.1 %copy-start.2 = (bf16[27,28,56]{2,1,0:T(8,128)(2,1)S(1)}, bf16[27,28,56]{2,1,0:T(8,128)(2,1)}, u32[]{:S(2)}) copy-start(bf16[27,28,56]{2,1,0:T(8,128)(2,1)} %w4.1) | copy-start | bytes 254020
  2.0 1.2 %copy-start.3 = (bf16[9,28,28]{2,1,0:T(8,128)(2,1)S(1)}, bf16[9,28,28]{2,1,0:T(8,128)(2,1)}, u32[]{:S(2)}) copy-start(bf16[9,28,28]{2,1,0:T(8,128)(2,1)} %w1.1) | copy-start | bytes 42340
  2.0 1.2 %copy-start.4 = (s32[32]{0:T(128)S(1)}, s32[32]{0:T(128)}, u32[]{:S(2)}) copy-start(s32[32]{0:T(128)} %first_block.3) | copy-start | bytes 388
  2.0 1.2 %copy-start.5 = (bf16[3,28]{1,0:T(4,128)(2,1)S(1)}, bf16[3,28]{1,0:T(4,128)(2,1)}, u32[]{:S(2)}) copy-start(bf16[3,28]{1,0:T(4,128)(2,1)} %hw.1) | copy-start | bytes 508
  2.1 1.2 %copy-start.6 = (s32[32]{0:T(128)S(1)}, s32[32]{0:T(128)}, u32[]{:S(2)}) copy-start(s32[32]{0:T(128)} %offset.1) | copy-start | bytes 388
  2.1 1.1 %copy-start.7 = (f32[28]{0:T(128)S(1)}, f32[28]{0:T(128)}, u32[]{:S(2)}) copy-start(f32[28]{0:T(128)} %param.18) | copy-start | bytes 340
  2.1 1.1 %copy-start.8 = (f32[28]{0:T(128)S(1)}, f32[28]{0:T(128)}, u32[]{:S(2)}) copy-start(f32[28]{0:T(128)} %param.20) | copy-start | bytes 340
  2.1 1.1 %copy-start.9 = (f32[28]{0:T(128)S(1)}, f32[28]{0:T(128)}, u32[]{:S(2)}) copy-start(f32[28]{0:T(128)} %param.22) | copy-start | bytes 340
  2.1 1.1 %copy-start.10 = (f32[28]{0:T(128)S(1)}, f32[28]{0:T(128)}, u32[]{:S(2)}) copy-start(f32[28]{0:T(128)} %param.24) | copy-start | bytes 340
  2.1 1.1 %copy-start.11 = (f32[3]{0:T(128)S(1)}, f32[3]{0:T(128)}, u32[]{:S(2)}) copy-start(f32[3]{0:T(128)} %param.26) | copy-start | bytes 40
  2.1 1.1 %copy-start.12 = (f32[1,128]{1,0:T(1,128)S(1)}, f32[1,128]{1,0:T(1,128)}, u32[]{:S(2)}) copy-start(f32[1,128]{1,0:T(1,128)} %constant.5.wy) | copy-start | bytes 1540

commit v2 on v1

--- a/solution.py
+++ b/solution.py
@@ -68,14 +68,30 @@
 
 def unet_kernel(
     owners,
-    first_block,
-    offset,
+    first_block_h,
+    offset_h,
     features,
     deep,
     w1,
     w2,
     w3,
     w4,
+    b1_h,
+    b2_h,
+    b3_h,
+    b4_h,
+    hw_h,
+    hb_h,
+    wy_h,
+    out,
+    first_block,
+    offset,
+    feat_v,
+    deep_v,
+    w1_v,
+    w2_v,
+    w3_v,
+    w4_v,
     b1,
     b2,
     b3,
@@ -83,13 +99,6 @@
     hw,
     hb,
     wy,
-    out,
-    feat_v,
-    deep_v,
-    w1_v,
-    w2_v,
-    w3_v,
-    w4_v,
     cells,
     xf,
     x1,
@@ -107,7 +116,7 @@
     head,
     sems,
 ):
-    chans, depth, along = feat_v.shape[0], feat_v.shape[1], feat_v.shape[2]
+    chans, along, depth = feat_v.shape[0], feat_v.shape[1], feat_v.shape[2]
     plane = depth * SLOT
     me = lax.axis_index("segment")
     patch = lax.axis_index("patch") * features.shape[0] + me
@@ -122,6 +131,15 @@
                 (deep.at[me], deep_v),
                 (w3, w3_v),
                 (w4, w4_v),
+                (b1_h, b1),
+                (b2_h, b2),
+                (b3_h, b3),
+                (b4_h, b4),
+                (hw_h, hw),
+                (hb_h, hb),
+                (wy_h, wy),
+                (first_block_h, first_block),
+                (offset_h, offset),
             ]
         )
     ]
@@ -141,18 +159,16 @@
     strip[...] = jnp.zeros(strip.shape, F32)
     head[...] = jnp.zeros(head.shape, F32)
     out[...] = jnp.zeros(out.shape, F32)
-    rows16 = 16
-    cells[chans * depth * rows16 :, :] = jnp.zeros(
-        (cells.shape[0] - chans * depth * rows16, LANES), F32
-    )
+    used = chans * along * depth
+    cells[used:, :] = jnp.zeros((cells.shape[0] - used, LANES), F32)
 
     def spread_cells(source):
         for c in range(chans):
-            for z in range(depth):
-                cells[pl.ds((c * depth + z) * rows16, along), :] = source[c, z].astype(F32)
+            for a in range(along):
+                cells[pl.ds((c * along + a) * depth, depth), :] = source[c, a].astype(F32)
 
     def gathered(z, a):
-        return cells[pl.ds(z * rows16 + a, SLOT, stride=depth * rows16), :]
+        return cells[pl.ds(a * depth + z, SLOT, stride=along * depth), :]
 
     def own(r):
         return r
@@ -164,6 +180,8 @@
             put_shifted(xf, z * high + (a + 1) * SLOT, gathered(z, a))
 
     copies[1].wait()
+    for c in copies[6:]:
+        c.wait()
     span = (GROUP + 2) * SLOT
     for dy in range(3):
         for da in range(3):
@@ -261,15 +279,22 @@
                     out[z * owners + owner, kind, pl.ds(cell, 1), :] = part[r : r + 1, :]
 
 
-def blend_kernel(owners, segments, first_block, mine, out):
+def blend_kernel(owners, segments, first_block_h, mine, out, first_block, sem):
+    copy = pltpu.make_async_copy(first_block_h, first_block, sem)
+    copy.start()
     owner = lax.axis_index("patch")
     out[...] = jnp.zeros(out.shape, F32)
+    copy.wait()
     for src in range(mine.shape[0]):
         patch = (src % owners) * segments + src // owners
         first = first_block[patch]
         ahead = lax.rem(owner - first + owners * CH_DEV, owners)
         index = jnp.minimum((first + ahead) // owners, CH_DEV - 1)
         out[index] += mine[src]
+
+
+def in_hbm(*arrays):
+    return [pltpu.with_memory_space_constraint(a, pltpu.HBM) for a in arrays]
 
 
 def per_device(
@@ -296,24 +321,32 @@
     assert along % GROUP == 0 and chans <= SLOT and depth * SLOT == LANES
     plane = depth * SLOT
     vmem = pl.BlockSpec(memory_space=pltpu.VMEM)
-    smem = pl.BlockSpec(memory_space=pltpu.SMEM)
-    hbm = pl.BlockSpec(memory_space=pl.ANY)
+    hbm = pl.BlockSpec(memory_space=pltpu.HBM)
     act = pltpu.VMEM((3, (along + 2) * plane, LANES), BF)
     taps = pltpu.VMEM((plane, 9 * LANES), BF)
     wy = jnp.asarray(bump(across)).reshape(1, across)
     slots = pl.pallas_call(
         functools.partial(unet_kernel, owners),
         out_shape=jax.ShapeDtypeStruct((segments * owners, kinds, CW, across), F32),
-        in_specs=[smem, smem] + [hbm] * 6 + [vmem] * 7,
+        in_specs=[hbm] * 15,
         out_specs=vmem,
         scratch_shapes=[
-            pltpu.VMEM((chans, depth, along, across), BF),
-            pltpu.VMEM((chans, depth, along, across), BF),
+            pltpu.SMEM(block_first.shape, jnp.int32),
+            pltpu.SMEM(block_first.shape, jnp.int32),
+            pltpu.VMEM((chans, along, depth, across), BF),
+            pltpu.VMEM((chans, along, depth, across), BF),
             pltpu.VMEM(weight_first.shape, BF),
             pltpu.VMEM(weight_second.shape, BF),
             pltpu.VMEM(weight_third.shape, BF),
             pltpu.VMEM(weight_fourth.shape, BF),
-            pltpu.VMEM((SLOT * depth * 16, LANES), F32),
+            pltpu.VMEM((1, chans), F32),
+            pltpu.VMEM((1, chans), F32),
+            pltpu.VMEM((1, chans), F32),
+            pltpu.VMEM((1, chans), F32),
+            pltpu.VMEM(head_weight.shape, BF),
+            pltpu.VMEM((1, kinds), F32),
+            pltpu.VMEM((1, across), F32),
+            pltpu.VMEM((SLOT * along * depth, LANES), F32),
             pltpu.VMEM((3, depth * (along + 2) * SLOT, LANES), BF),
             act,
             act,
@@ -328,14 +361,15 @@
             pltpu.VMEM((5, 9, SLOT, LANES), F32),
             pltpu.VMEM((8, LANES), F32),
             pltpu.VMEM((4 * depth, LANES), F32),
-            pltpu.SemaphoreType.DMA((6,)),
+            pltpu.SemaphoreType.DMA((15,)),
         ],
         compiler_params=pltpu.CompilerParams(vmem_limit_bytes=48 * 2**20),
     )(
+        *in_hbm(
         block_first,
         block_offset,
-        features,
-        deep_path,
+        features.transpose(0, 1, 3, 2, 4),
+        deep_path.transpose(0, 1, 3, 2, 4),
         weight_first,
         weight_second,
         weight_third,
@@ -347,14 +381,16 @@
         head_weight,
         head_bias.reshape(1, kinds),
         wy,
+        )
     )
     mine = lax.all_to_all(slots, ("segment", "patch"), split_axis=0, concat_axis=0, tiled=True)
     blended = pl.pallas_call(
         functools.partial(blend_kernel, owners, segments),
         out_shape=jax.ShapeDtypeStruct((CH_DEV, kinds, CW, across), F32),
-        in_specs=[smem, vmem],
+        in_specs=[hbm, vmem],
         out_specs=vmem,
-    )(block_first, mine)
+        scratch_shapes=[pltpu.SMEM(block_first.shape, jnp.int32), pltpu.SemaphoreType.DMA(())],
+    )(*in_hbm(block_first), mine)
     return blended.reshape(CH_DEV, 1, kinds, 1, CW, across)
 
 

time: 30.9 us -> 26.7 us (0.86)
  local copies, waits for them, and re-layouts: 3.1 us -> 0 us
  Pallas kernels: 11.7 us -> 10.8 us
    unnamed x30 -> x0, local copies, waits for them, and re-layouts: 3.1 us -> none
    pallas_call x1, Pallas kernels: 9.88 us -> 8.34 us  [per_device(): pl.pallas_call(functools.partial(unet_kernel, owners), out_shape=jax.Shap...]
    pallas_call x1, Pallas kernels: 1.83 us -> 2.49 us  [per_device(): pl.pallas_call(functools.partial(blend_kernel, owners, segments), out_sha...]
where the time goes in v2:
time: 26.7 us; the launch traced here: 26.6 us
  blocking collectives  15.7 us (59%)
  Pallas kernels  10.8 us (40%)
    all_to_all x1, blocking collectives, per_device(): lax.all_to_all(slots, ('segment', 'patch'), split_axis=0, concat_axis=0,...  15.7 us
    pallas_call x1, Pallas kernels, per_device(): pl.pallas_call(functools.partial(unet_kernel, owners), out_shape=jax.Shap...  8.34 us
    pallas_call x1, Pallas kernels, per_device(): pl.pallas_call(functools.partial(blend_kernel, owners, segments), out_sha...  2.49 us

profile of v2, /device:TPU:0, one launch (start us, length us, event | category | flops | bytes accessed | tf_op | source)
XLA Modules:
  0.0 26.6 jit_solution(6708394329188921103)
XLA Ops:
  0.0 8.3 %shard_map.145 = f32[32,3,4,128]{3,2,1,0:T(4,128)S(1)} custom-call(s32[32]{0:T(128)} %first_block_h.3, s32[32]{0:T(128)} %offset_h.1, bf16[4,28,12,4,128]{4,3,2,1,0:T(4,128)(2,1)} %bitcast.10, bf16[4,28,12,4,128]{4,3,2,1,0:T(4,128)(2,1)} %bitcast.11, bf16[9,28,28]{2,1,0:T(8,128)(2,1)} %w1.1, bf16[27,28,28]{2,1,0:T(8,128)(2,1)} %w2.1, ...), custom_call_target="tpu_custom_call" | custom-call | tf_op jit(solution)/shard_map/pallas_call | solution.py:328
  8.3 15.7 %all_to_all.5.mine = f32[32,3,4,128]{3,2,1,0:T(4,128)} all-to-all(f32[32,3,4,128]{3,2,1,0:T(4,128)S(1)} %shard_map.145), channel_id=1, replica_groups=mesh['segment'=4,'patch'=8] {'segment','patch'}, dimensions={0} | all-to-all | bytes 393216 | tf_op jit(solution)/shard_map/all_to_all | solution.py:386
  24.1 2.5 %shard_map.146 = f32[8,3,4,128]{3,2,1,0:T(4,128)} custom-call(s32[32]{0:T(128)} %first_block_h.3, f32[32,3,4,128]{3,2,1,0:T(4,128)} %all_to_all.5.mine), custom_call_target="tpu_custom_call" | custom-call | tf_op jit(solution)/shard_map/pallas_call | solution.py:387

commit v3 on v2

--- a/solution.py
+++ b/solution.py
@@ -14,6 +14,7 @@
 KMAX = 4
 LANES = 128
 SLOT = 32
+ROWS = 16
 GROUP = 4
 BF = jnp.bfloat16
 F32 = jnp.float32
@@ -31,31 +32,30 @@
 def put_shifted(act, row, value):
     rows = value.shape[0]
     lane = lane_index(rows)
-    act[1, pl.ds(row, rows), :] = value.astype(BF)
-    act[0, pl.ds(row, rows), :] = jnp.where(lane == 0, 0.0, pltpu.roll(value, 1, 1)).astype(BF)
-    act[2, pl.ds(row, rows), :] = jnp.where(
-        lane == LANES - 1, 0.0, pltpu.roll(value, LANES - 1, 1)
-    ).astype(BF)
-
-
-def build_taps(weight, low, chans, strip, big, depth):
+    value = value.astype(BF)
+    zero = jnp.zeros(value.shape, BF)
+    act[1, pl.ds(row, rows), :] = value
+    act[0, pl.ds(row, rows), :] = jnp.where(lane == 0, zero, pltpu.roll(value, 1, 1))
+    act[2, pl.ds(row, rows), :] = jnp.where(lane == LANES - 1, zero, pltpu.roll(value, LANES - 1, 1))
+
+
+def build_block(weight, low, chans, strip, big, depth, dy, da):
     lane = lane_index(SLOT)
-    for dy in range(3):
-        for da in range(3):
-            k = dy * 3 + da
-            for dz in range(3):
-                strip[k, 0:chans, dz * SLOT : dz * SLOT + chans] = weight[
-                    9 * dz + 3 * da + dy, :, low : low + chans
-                ].astype(F32)
-            base = strip[k]
-            for z in range(depth):
-                shift = ((z - 1) * SLOT) % LANES
-                moved = pltpu.roll(base, shift, 1) if shift else base
-                if z == 0:
-                    moved = jnp.where(lane < LANES - SLOT, moved, 0.0)
-                if z == depth - 1:
-                    moved = jnp.where(lane >= SLOT, moved, 0.0)
-                big[z * SLOT : (z + 1) * SLOT, k * LANES : (k + 1) * LANES] = moved.astype(BF)
+    zero = jnp.zeros((SLOT, LANES), BF)
+    k = dy * 3 + da
+    for dz in range(3):
+        strip[k, 0:chans, dz * SLOT : dz * SLOT + chans] = weight[
+            9 * dz + 3 * da + dy, :, low : low + chans
+        ]
+    base = strip[k]
+    for z in range(depth):
+        shift = ((z - 1) * SLOT) % LANES
+        moved = pltpu.roll(base, shift, 1) if shift else base
+        if z == 0:
+            moved = jnp.where(lane < LANES - SLOT, moved, zero)
+        if z == depth - 1:
+            moved = jnp.where(lane >= SLOT, moved, zero)
+        big[z * SLOT : (z + 1) * SLOT, k * LANES : (k + 1) * LANES] = moved
 
 
 def column(row_ref, pad, rows, pick):
@@ -84,6 +84,7 @@
     hb_h,
     wy_h,
     out,
+    adder,
     first_block,
     offset,
     feat_v,
@@ -114,6 +115,7 @@
     strip,
     pad,
     head,
+    canvas,
     sems,
 ):
     chans, along, depth = feat_v.shape[0], feat_v.shape[1], feat_v.shape[2]
@@ -156,9 +158,9 @@
             xf[dy, z * high : z * high + SLOT, :] = jnp.zeros((SLOT, LANES), BF)
             xf[dy, (z + 1) * high - SLOT : (z + 1) * high, :] = jnp.zeros((SLOT, LANES), BF)
     m1[...] = jnp.zeros(m1.shape, F32)
-    strip[...] = jnp.zeros(strip.shape, F32)
+    strip[...] = jnp.zeros(strip.shape, BF)
     head[...] = jnp.zeros(head.shape, F32)
-    out[...] = jnp.zeros(out.shape, F32)
+    canvas[...] = jnp.zeros(canvas.shape, F32)
     used = chans * along * depth
     cells[used:, :] = jnp.zeros((cells.shape[0] - used, LANES), F32)
 
@@ -172,6 +174,23 @@
 
     def own(r):
         return r
+
+    def make_adder():
+        row = lax.broadcasted_iota(jnp.int32, (adder.shape[0], LANES), 0)
+        lane = lane_index(adder.shape[0])
+        here = lax.axis_index("patch")
+        each = LANES // ROWS
+        for block in range(adder.shape[1] // LANES):
+            index = jnp.full((1, LANES), -1, jnp.int32)
+            thin = lax.broadcasted_iota(jnp.int32, (1, LANES), 1)
+            for j in range(each):
+                src = block * each + j
+                first = first_block[(src % owners) * features.shape[0] + src // owners]
+                ahead = lax.rem(here - first + owners * CH_DEV, owners)
+                found = jnp.where(ahead < KMAX, (first + ahead) // owners, -1)
+                index = jnp.where(thin // ROWS == j, found, index)
+            keep = (row // ROWS == index) & (row % ROWS == lane % ROWS)
+            adder[:, block * LANES : (block + 1) * LANES] = jnp.where(keep, 1.0, 0.0).astype(BF)
 
     copies[0].wait()
     spread_cells(feat_v)
@@ -179,9 +198,9 @@
         for a in range(along):
             put_shifted(xf, z * high + (a + 1) * SLOT, gathered(z, a))
 
-    copies[1].wait()
-    for c in copies[6:]:
+    for c in copies[1:]:
         c.wait()
+    make_adder()
     span = (GROUP + 2) * SLOT
     for dy in range(3):
         for da in range(3):
@@ -196,7 +215,22 @@
         tile = jnp.broadcast_to(col, (SLOT, LANES))
         return jnp.concatenate([tile] * copies_of, axis=0)
 
+    def matrix_tasks(weight, low, index, big):
+        return [
+            functools.partial(
+                build_block, weight, low, chans, strip.at[index], big, depth, dy, da
+            )
+            for dy in range(3)
+            for da in range(3)
+        ]
+
+    def run(tasks, step, steps):
+        for task in tasks[len(tasks) * step // steps : len(tasks) * (step + 1) // steps]:
+            task()
+
     bias = bias_rows(b1, GROUP)
+    bias2, bias3, bias4 = (bias_rows(b, depth) for b in (b2, b3, b4))
+    tasks = matrix_tasks(w2_v, 0, 0, m2)
     for z in range(depth):
         for pair in range(0, along // GROUP):
             rhs = jnp.concatenate(
@@ -210,6 +244,7 @@
                     (1 + pair * GROUP + a) * plane + z * SLOT,
                     got[a * SLOT : (a + 1) * SLOT],
                 )
+            run(tasks, z * (along // GROUP) + pair, depth * (along // GROUP))
 
     def window_of(act, a):
         return jnp.concatenate([act[dy, pl.ds(a * plane, 3 * plane), :] for dy in range(3)], axis=0)
@@ -224,30 +259,24 @@
         wide = jnp.concatenate([bias, bias], axis=1)
         return jnp.maximum(got + wide, 0.0)
 
-    def layer(mats, acts, bias, result):
+    def layer(mats, acts, bias, result, tasks):
         for a in range(0, along, 2):
             got = conv(mats, acts, bias, a)
+            run(tasks, a // 2, along // 2)
             for h in range(2):
                 put_shifted(result, (1 + a + h) * plane, got[:, h * LANES : (h + 1) * LANES])
 
-    copies[2].wait()
-    build_taps(w2_v, 0, chans, strip.at[0], m2, depth)
-    layer([m2], [x1], bias_rows(b2, depth), x2)
-
-    copies[3].wait()
+    def deep_rows(a):
+        for z in range(depth):
+            put_shifted(xd, (a + 1) * plane + z * SLOT, gathered(z, a))
+
     spread_cells(deep_v)
-    for z in range(depth):
-        for a in range(along):
-            put_shifted(xd, (a + 1) * plane + z * SLOT, gathered(z, a))
-    copies[4].wait()
-    build_taps(w3_v, 0, chans, strip.at[1], m3s, depth)
-    build_taps(w3_v, chans, chans, strip.at[2], m3d, depth)
-    layer([m3s, m3d], [x2, xd], bias_rows(b3, depth), x3)
-
-    copies[5].wait()
-    build_taps(w4_v, 0, chans, strip.at[3], m4t, depth)
-    build_taps(w4_v, chans, chans, strip.at[4], m4f, depth)
-    bias = bias_rows(b4, depth)
+    tasks = matrix_tasks(w3_v, 0, 1, m3s) + matrix_tasks(w3_v, chans, 2, m3d)
+    tasks += [functools.partial(deep_rows, a) for a in range(along)]
+    layer([m2], [x1], bias2, x2, tasks)
+    tasks = matrix_tasks(w4_v, 0, 3, m4t) + matrix_tasks(w4_v, chans, 4, m4f)
+    layer([m3s, m3d], [x2, xd], bias3, x3, tasks)
+    bias = bias4
     kinds = hw.shape[0]
     tap = hw[...].astype(F32)
     for z in range(depth):
@@ -276,21 +305,19 @@
             for z in range(depth):
                 for kind in range(kinds):
                     r = z * 4 + kind
-                    out[z * owners + owner, kind, pl.ds(cell, 1), :] = part[r : r + 1, :]
-
-
-def blend_kernel(owners, segments, first_block_h, mine, out, first_block, sem):
-    copy = pltpu.make_async_copy(first_block_h, first_block, sem)
-    copy.start()
-    owner = lax.axis_index("patch")
-    out[...] = jnp.zeros(out.shape, F32)
-    copy.wait()
-    for src in range(mine.shape[0]):
-        patch = (src % owners) * segments + src // owners
-        first = first_block[patch]
-        ahead = lax.rem(owner - first + owners * CH_DEV, owners)
-        index = jnp.minimum((first + ahead) // owners, CH_DEV - 1)
-        out[index] += mine[src]
+                    to = (z * owners + owner) * ROWS + kind * CW + cell
+                    canvas[pl.ds(to, 1), :] = part[r : r + 1, :]
+    for slot in range(out.shape[0]):
+        out[slot] = canvas[slot * ROWS : (slot + 1) * ROWS, :].astype(BF)
+
+
+def blend_kernel(adder, mine, out):
+    rows = mine[...].reshape(mine.shape[0] * ROWS, LANES)
+    total = jnp.dot(adder[...], rows, preferred_element_type=F32)
+    for i in range(out.shape[0]):
+        for kind in range(out.shape[1]):
+            lo = i * ROWS + kind * CW
+            out[i, kind] = total[lo : lo + CW, :]
 
 
 def in_hbm(*arrays):
@@ -318,18 +345,21 @@
     count, chans, depth, along, across = features.shape
     kinds = head_weight.shape[0]
     assert count == segments and depth == segments and across == LANES
-    assert along % GROUP == 0 and chans <= SLOT and depth * SLOT == LANES
+    assert along % GROUP == 0 and kinds * CW <= ROWS and chans <= SLOT and depth * SLOT == LANES
     plane = depth * SLOT
     vmem = pl.BlockSpec(memory_space=pltpu.VMEM)
     hbm = pl.BlockSpec(memory_space=pltpu.HBM)
     act = pltpu.VMEM((3, (along + 2) * plane, LANES), BF)
     taps = pltpu.VMEM((plane, 9 * LANES), BF)
     wy = jnp.asarray(bump(across)).reshape(1, across)
-    slots = pl.pallas_call(
+    slots, adder = pl.pallas_call(
         functools.partial(unet_kernel, owners),
-        out_shape=jax.ShapeDtypeStruct((segments * owners, kinds, CW, across), F32),
+        out_shape=(
+            jax.ShapeDtypeStruct((segments * owners, ROWS, across), BF),
+            jax.ShapeDtypeStruct((CH_DEV * ROWS, segments * owners * ROWS), BF),
+        ),
         in_specs=[hbm] * 15,
-        out_specs=vmem,
+        out_specs=(vmem, vmem),
         scratch_shapes=[
             pltpu.SMEM(block_first.shape, jnp.int32),
             pltpu.SMEM(block_first.shape, jnp.int32),
@@ -358,9 +388,10 @@
             taps,
             taps,
             taps,
-            pltpu.VMEM((5, 9, SLOT, LANES), F32),
+            pltpu.VMEM((5, 9, SLOT, LANES), BF),
             pltpu.VMEM((8, LANES), F32),
             pltpu.VMEM((4 * depth, LANES), F32),
+            pltpu.VMEM((segments * owners * ROWS, LANES), F32),
             pltpu.SemaphoreType.DMA((15,)),
         ],
         compiler_params=pltpu.CompilerParams(vmem_limit_bytes=48 * 2**20),
@@ -385,12 +416,11 @@
     )
     mine = lax.all_to_all(slots, ("segment", "patch"), split_axis=0, concat_axis=0, tiled=True)
     blended = pl.pallas_call(
-        functools.partial(blend_kernel, owners, segments),
+        blend_kernel,
         out_shape=jax.ShapeDtypeStruct((CH_DEV, kinds, CW, across), F32),
-        in_specs=[hbm, vmem],
+        in_specs=[vmem, vmem],
         out_specs=vmem,
-        scratch_shapes=[pltpu.SMEM(block_first.shape, jnp.int32), pltpu.SemaphoreType.DMA(())],
-    )(*in_hbm(block_first), mine)
+    )(adder, mine)
     return blended.reshape(CH_DEV, 1, kinds, 1, CW, across)
 
 

time: 26.7 us -> 24.3 us (0.910)
  Pallas kernels: 10.8 us -> 8.59 us
  blocking collectives: 15.7 us -> 14.9 us
  local copies, waits for them, and re-layouts: 0 us -> 0.63 us
    pallas_call x2, Pallas kernels: 10.8 us -> 8.59 us  [the longest x1 6.83 us: per_device(): pl.pallas_call(functools.partial(unet_kernel, owners), out_shape=(jax.Sha...]
    all_to_all x1, blocking collectives: 15.7 us -> 14.9 us  [per_device(): lax.all_to_all(slots, ('segment', 'patch'), split_axis=0, concat_axis=0,...]
    unnamed x0 -> x2, local copies, waits for them, and re-layouts: none -> 0.63 us
where the time goes in v3:
time: 24.3 us; the launch traced here: 24.2 us
  blocking collectives  14.9 us (61%)
  Pallas kernels  8.59 us (35%)
  local copies, waits for them, and re-layouts  0.63 us (3%)
    all_to_all x1, blocking collectives, per_device(): lax.all_to_all(slots, ('segment', 'patch'), split_axis=0, concat_axis=0,...  14.9 us
    pallas_call x1, Pallas kernels, per_device(): pl.pallas_call(functools.partial(unet_kernel, owners), out_shape=(jax.Sha...  6.83 us
    pallas_call x1, Pallas kernels, per_device(): pl.pallas_call(blend_kernel, out_shape=jax.ShapeDtypeStruct((CH_DEV, kind...  1.76 us
    unnamed x2, local copies, waits for them, and re-layouts  0.63 us

profile of v3, /device:TPU:0, one launch (start us, length us, event | category | flops | bytes accessed | tf_op | source)
XLA Modules:
  0.0 24.2 jit_solution(8804271438360627362)
XLA Ops:
  0.0 6.8 %shard_map.145 = (bf16[32,16,128]{2,1,0:T(8,128)(2,1)S(1)}, bf16[128,512]{1,0:T(8,128)(2,1)S(1)}) custom-call(s32[32]{0:T(128)} %first_block_h.1, s32[32]{0:T(128)} %offset_h.1, bf16[4,28,12,4,128]{4,3,2,1,0:T(4,128)(2,1)} %bitcast.10, bf16[4,28,12,4,128]{4,3,2,1,0:T(4,128)(2,1)} %bitcast.11, bf16[9,28,28]{2,1,0:T(8,128)(2,1)} %w1.1, ...), custom_call_target="tpu_custom_call" | custom-call | tf_op jit(solution)/shard_map/pallas_call | solution.py:355
  6.8 0.0 copy-start
  6.8 0.6 %copy-done = bf16[128,512]{1,0:T(8,128)(2,1)} copy-done((bf16[128,512]{1,0:T(8,128)(2,1)}, bf16[128,512]{1,0:T(8,128)(2,1)S(1)}, u32[]{:S(2)}) %copy-start) | copy-done | bytes 131096
  7.5 14.9 %all_to_all.5.mine = bf16[32,16,128]{2,1,0:T(8,128)(2,1)} all-to-all(bf16[32,16,128]{2,1,0:T(8,128)(2,1)S(1)} %get-tuple-element.8), channel_id=1, replica_groups=mesh['segment'=4,'patch'=8] {'segment','patch'}, dimensions={0} | all-to-all | bytes 262144 | tf_op jit(solution)/shard_map/all_to_all | solution.py:417
  22.4 1.8 %shard_map.146 = f32[8,3,4,128]{3,2,1,0:T(4,128)} custom-call(bf16[128,512]{1,0:T(8,128)(2,1)} %copy-done, bf16[32,16,128]{2,1,0:T(8,128)(2,1)} %all_to_all.5.mine), custom_call_target="tpu_custom_call" | custom-call | tf_op jit(solution)/shard_map/pallas_call | solution.py:418
Async XLA Ops:
  6.8 0.6 %copy-start = (bf16[128,512]{1,0:T(8,128)(2,1)}, bf16[128,512]{1,0:T(8,128)(2,1)S(1)}, u32[]{:S(2)}) copy-start(bf16[128,512]{1,0:T(8,128)(2,1)S(1)} %get-tuple-element.7.adder) | copy-start | bytes 393220

commit v4 on v3

--- a/solution.py
+++ b/solution.py
@@ -320,8 +320,8 @@
             out[i, kind] = total[lo : lo + CW, :]
 
 
-def in_hbm(*arrays):
-    return [pltpu.with_memory_space_constraint(a, pltpu.HBM) for a in arrays]
+def held_in(space, *arrays):
+    return [pltpu.with_memory_space_constraint(a, space) for a in arrays]
 
 
 def per_device(
@@ -396,7 +396,8 @@
         ],
         compiler_params=pltpu.CompilerParams(vmem_limit_bytes=48 * 2**20),
     )(
-        *in_hbm(
+        *held_in(
+            pltpu.HBM,
         block_first,
         block_offset,
         features.transpose(0, 1, 3, 2, 4),
@@ -420,7 +421,7 @@
         out_shape=jax.ShapeDtypeStruct((CH_DEV, kinds, CW, across), F32),
         in_specs=[vmem, vmem],
         out_specs=vmem,
-    )(adder, mine)
+    )(*held_in(pltpu.VMEM, adder, mine))
     return blended.reshape(CH_DEV, 1, kinds, 1, CW, across)
 
 

time: 24.3 us -> 22.6 us (0.930)
  Pallas kernels: 8.59 us -> 7.62 us
  local copies, waits for them, and re-layouts: 0.63 us -> 0 us
    pallas_call x1, Pallas kernels: 1.76 us -> 0.8 us  [per_device(): pl.pallas_call(blend_kernel, out_shape=jax.ShapeDtypeStruct((CH_DEV, kind...]
    unnamed x2 -> x0, local copies, waits for them, and re-layouts: 0.63 us -> none
where the time goes in v4:
time: 22.6 us; the launch traced here: 22.5 us
  blocking collectives  14.8 us (65%)
  Pallas kernels  7.62 us (34%)
    all_to_all x1, blocking collectives, per_device(): lax.all_to_all(slots, ('segment', 'patch'), split_axis=0, concat_axis=0,...  14.8 us
    pallas_call x1, Pallas kernels, per_device(): pl.pallas_call(functools.partial(unet_kernel, owners), out_shape=(jax.Sha...  6.83 us
    pallas_call x1, Pallas kernels, per_device(): pl.pallas_call(blend_kernel, out_shape=jax.ShapeDtypeStruct((CH_DEV, kind...  0.8 us

profile of v4, /device:TPU:0, one launch (start us, length us, event | category | flops | bytes accessed | tf_op | source)
XLA Modules:
  0.0 22.5 jit_solution(1318444691810041834)
XLA Ops:
  0.0 6.8 %shard_map.145 = (bf16[32,16,128]{2,1,0:T(8,128)(2,1)S(1)}, bf16[128,512]{1,0:T(8,128)(2,1)S(1)}) custom-call(s32[32]{0:T(128)} %first_block_h.1, s32[32]{0:T(128)} %offset_h.1, bf16[4,28,12,4,128]{4,3,2,1,0:T(4,128)(2,1)} %bitcast.10, bf16[4,28,12,4,128]{4,3,2,1,0:T(4,128)(2,1)} %bitcast.11, bf16[9,28,28]{2,1,0:T(8,128)(2,1)} %w1.1, ...), custom_call_target="tpu_custom_call" | custom-call | tf_op jit(solution)/shard_map/pallas_call | solution.py:355
  6.8 14.8 %all_to_all.5.mine = bf16[32,16,128]{2,1,0:T(8,128)(2,1)S(1)} all-to-all(bf16[32,16,128]{2,1,0:T(8,128)(2,1)S(1)} %get-tuple-element.8), channel_id=1, replica_groups=mesh['segment'=4,'patch'=8] {'segment','patch'}, dimensions={0} | all-to-all | bytes 262144 | tf_op jit(solution)/shard_map/all_to_all | solution.py:418
  21.7 0.8 %shard_map.146 = f32[8,3,4,128]{3,2,1,0:T(4,128)} custom-call(bf16[128,512]{1,0:T(8,128)(2,1)S(1)} %get-tuple-element.7.adder, bf16[32,16,128]{2,1,0:T(8,128)(2,1)S(1)} %all_to_all.5.mine), custom_call_target="tpu_custom_call" | custom-call | tf_op jit(solution)/shard_map/pallas_call | solution.py:419

commit v5 on v4

--- a/solution.py
+++ b/solution.py
@@ -14,6 +14,7 @@
 KMAX = 4
 LANES = 128
 SLOT = 32
+TILE = 16
 ROWS = 16
 GROUP = 4
 BF = jnp.bfloat16
@@ -29,33 +30,70 @@
     return lax.broadcasted_iota(jnp.int32, (rows, LANES), 1)
 
 
+def lane_mask(low, high):
+    lane = lane_index(TILE)
+    return jnp.where((lane >= low) & (lane < high), 1.0, 0.0).astype(BF)
+
+
+def masked(value, tile):
+    rows = value.shape[0]
+    return (value.reshape(rows // TILE, TILE, LANES) * tile[None]).reshape(rows, LANES)
+
+
 def put_shifted(act, row, value):
     rows = value.shape[0]
-    lane = lane_index(rows)
     value = value.astype(BF)
-    zero = jnp.zeros(value.shape, BF)
     act[1, pl.ds(row, rows), :] = value
-    act[0, pl.ds(row, rows), :] = jnp.where(lane == 0, zero, pltpu.roll(value, 1, 1))
-    act[2, pl.ds(row, rows), :] = jnp.where(lane == LANES - 1, zero, pltpu.roll(value, LANES - 1, 1))
-
-
-def build_block(weight, low, chans, strip, big, depth, dy, da):
-    lane = lane_index(SLOT)
-    zero = jnp.zeros((SLOT, LANES), BF)
-    k = dy * 3 + da
+    act[0, pl.ds(row, rows), :] = masked(pltpu.roll(value, 1, 1), lane_mask(1, LANES))
+    act[2, pl.ds(row, rows), :] = masked(
+        pltpu.roll(value, LANES - 1, 1), lane_mask(0, LANES - 1)
+    )
+
+
+def turned(value, lanes):
+    return pltpu.roll(value, lanes % LANES, 1) if lanes % LANES else value
+
+
+def pad_taps(weight, padded):
+    taps, rows, cols = weight.shape
+    for t in range(taps):
+        padded[t, 0:rows, 0:cols] = weight[t]
+
+
+def build_bands(padded, low, chans, wide, big, depth, da):
+    parts = []
     for dz in range(3):
-        strip[k, 0:chans, dz * SLOT : dz * SLOT + chans] = weight[
-            9 * dz + 3 * da + dy, :, low : low + chans
-        ]
-    base = strip[k]
+        taps = padded[9 * dz + 3 * da : 9 * dz + 3 * da + 3].reshape(3 * SLOT, LANES)
+        if low or wide:
+            taps = masked(taps, lane_mask(low, low + chans))
+        parts.append(turned(taps, dz * SLOT - low))
+    base = parts[0] + parts[1] + parts[2]
     for z in range(depth):
-        shift = ((z - 1) * SLOT) % LANES
-        moved = pltpu.roll(base, shift, 1) if shift else base
+        moved = turned(base, (z - 1) * SLOT)
         if z == 0:
-            moved = jnp.where(lane < LANES - SLOT, moved, zero)
+            moved = masked(moved, lane_mask(0, LANES - SLOT))
         if z == depth - 1:
-            moved = jnp.where(lane >= SLOT, moved, zero)
-        big[z * SLOT : (z + 1) * SLOT, k * LANES : (k + 1) * LANES] = moved
+            moved = masked(moved, lane_mask(SLOT, LANES))
+        for dy in range(3):
+            k = da * 3 + dy
+            big[z * SLOT : (z + 1) * SLOT, k * LANES : (k + 1) * LANES] = moved[
+                dy * SLOT : (dy + 1) * SLOT
+            ]
+
+
+def build_first(padded, big):
+    parts = [padded[3 * da : 3 * da + 3].reshape(3 * SLOT, LANES) for da in range(3)]
+    base = parts[0] + turned(parts[1], SLOT) + turned(parts[2], 2 * SLOT)
+    for a in range(GROUP):
+        moved = turned(base, a * SLOT)
+        wide = masked(moved, lane_mask(a * SLOT, LANES))
+        rest = masked(moved, lane_mask(0, (a - 1) * SLOT))
+        rows = slice(a * SLOT, (a + 1) * SLOT)
+        for dy in range(3):
+            big[rows, dy * LANES : (dy + 1) * LANES] = wide[dy * SLOT : (dy + 1) * SLOT]
+        half = [rest[dy * SLOT : (dy + 1) * SLOT] for dy in range(3)]
+        big[rows, 3 * LANES : 4 * LANES] = half[0] + turned(half[1], LANES // 2)
+        big[rows, 4 * LANES : 5 * LANES] = half[2]
 
 
 def column(row_ref, pad, rows, pick):
@@ -112,7 +150,10 @@
     m3d,
     m4t,
     m4f,
-    strip,
+    p1,
+    p2,
+    p3,
+    p4,
     pad,
     head,
     canvas,
@@ -157,8 +198,8 @@
         for z in range(depth):
             xf[dy, z * high : z * high + SLOT, :] = jnp.zeros((SLOT, LANES), BF)
             xf[dy, (z + 1) * high - SLOT : (z + 1) * high, :] = jnp.zeros((SLOT, LANES), BF)
-    m1[...] = jnp.zeros(m1.shape, F32)
-    strip[...] = jnp.zeros(strip.shape, BF)
+    for padded in (p1, p2, p3, p4):
+        padded[...] = jnp.zeros(padded.shape, BF)
     head[...] = jnp.zeros(head.shape, F32)
     canvas[...] = jnp.zeros(canvas.shape, F32)
     used = chans * along * depth
@@ -198,29 +239,23 @@
         for a in range(along):
             put_shifted(xf, z * high + (a + 1) * SLOT, gathered(z, a))
 
-    for c in copies[1:]:
+    copies[1].wait()
+    pad_taps(w1_v, p1)
+    build_first(p1, m1)
+    for c in copies[2:]:
         c.wait()
     make_adder()
-    span = (GROUP + 2) * SLOT
-    for dy in range(3):
-        for da in range(3):
-            tap = w1_v[da * 3 + dy].astype(F32)
-            for a in range(GROUP):
-                lo = dy * span + (a + da) * SLOT
-                m1[a * SLOT : a * SLOT + chans, lo : lo + chans] = tap
-    m1_b = m1[...].astype(BF)
+    for weight, padded in ((w2_v, p2), (w3_v, p3), (w4_v, p4)):
+        pad_taps(weight, padded)
 
     def bias_rows(ref, copies_of):
         col = column(ref, pad, SLOT, own)
         tile = jnp.broadcast_to(col, (SLOT, LANES))
         return jnp.concatenate([tile] * copies_of, axis=0)
 
-    def matrix_tasks(weight, low, index, big):
+    def matrix_tasks(padded, low, wide, big):
         return [
-            functools.partial(
-                build_block, weight, low, chans, strip.at[index], big, depth, dy, da
-            )
-            for dy in range(3)
+            functools.partial(build_bands, padded, low, chans, wide, big, depth, da)
             for da in range(3)
         ]
 
@@ -230,24 +265,33 @@
 
     bias = bias_rows(b1, GROUP)
     bias2, bias3, bias4 = (bias_rows(b, depth) for b in (b2, b3, b4))
-    tasks = matrix_tasks(w2_v, 0, 0, m2)
-    for z in range(depth):
-        for pair in range(0, along // GROUP):
-            rhs = jnp.concatenate(
-                [xf[dy, pl.ds(z * high + pair * GROUP * SLOT, span), :] for dy in range(3)], axis=0
-            )
-            got = jnp.dot(m1_b, rhs, preferred_element_type=F32)
-            got = jnp.maximum(got + bias, 0.0)
+    tasks = matrix_tasks(p2, 0, False, m2)
+    columns = [(z, group) for z in range(depth) for group in range(along // GROUP)]
+
+    def first_window(z, group):
+        low = z * high + group * GROUP * SLOT
+        pieces = [xf[dy, pl.ds(low, LANES), :] for dy in range(3)]
+        pieces += [xf[dy, pl.ds(low + LANES, LANES // 2), :] for dy in range(3)]
+        return jnp.concatenate(pieces, axis=0)
+
+    for pair in range(0, len(columns), 2):
+        rhs = jnp.concatenate([first_window(*c) for c in columns[pair : pair + 2]], axis=1)
+        got = jnp.dot(m1[:, 0 : rhs.shape[0]], rhs, preferred_element_type=F32)
+        run(tasks, pair // 2, len(columns) // 2)
+        for h, (z, group) in enumerate(columns[pair : pair + 2]):
+            part = jnp.maximum(got[:, h * LANES : (h + 1) * LANES] + bias, 0.0)
             for a in range(GROUP):
                 put_shifted(
                     x1,
-                    (1 + pair * GROUP + a) * plane + z * SLOT,
-                    got[a * SLOT : (a + 1) * SLOT],
+                    (1 + group * GROUP + a) * plane + z * SLOT,
+                    part[a * SLOT : (a + 1) * SLOT],
                 )
-            run(tasks, z * (along // GROUP) + pair, depth * (along // GROUP))
 
     def window_of(act, a):
-        return jnp.concatenate([act[dy, pl.ds(a * plane, 3 * plane), :] for dy in range(3)], axis=0)
+        return jnp.concatenate(
+            [act[dy, pl.ds((a + da) * plane, plane), :] for da in range(3) for dy in range(3)],
+            axis=0,
+        )
 
     def conv(mats, acts, bias, a):
         matrix = jnp.concatenate([m[...] for m in mats], axis=1) if len(mats) > 1 else mats[0][...]
@@ -271,10 +315,10 @@
             put_shifted(xd, (a + 1) * plane + z * SLOT, gathered(z, a))
 
     spread_cells(deep_v)
-    tasks = matrix_tasks(w3_v, 0, 1, m3s) + matrix_tasks(w3_v, chans, 2, m3d)
+    tasks = matrix_tasks(p3, 0, True, m3s) + matrix_tasks(p3, chans, True, m3d)
     tasks += [functools.partial(deep_rows, a) for a in range(along)]
     layer([m2], [x1], bias2, x2, tasks)
-    tasks = matrix_tasks(w4_v, 0, 3, m4t) + matrix_tasks(w4_v, chans, 4, m4f)
+    tasks = matrix_tasks(p4, 0, True, m4t) + matrix_tasks(p4, chans, True, m4f)
     layer([m3s, m3d], [x2, xd], bias3, x3, tasks)
     bias = bias4
     kinds = hw.shape[0]
@@ -382,13 +426,16 @@
             act,
             act,
             act,
-            pltpu.VMEM((GROUP * SLOT, 3 * (GROUP + 2) * SLOT), F32),
+            pltpu.VMEM((GROUP * SLOT, 5 * LANES), BF),
             taps,
             taps,
             taps,
             taps,
             taps,
-            pltpu.VMEM((5, 9, SLOT, LANES), BF),
+            pltpu.VMEM((9, SLOT, LANES), BF),
+            pltpu.VMEM((27, SLOT, LANES), BF),
+            pltpu.VMEM((27, SLOT, LANES), BF),
+            pltpu.VMEM((27, SLOT, LANES), BF),
             pltpu.VMEM((8, LANES), F32),
             pltpu.VMEM((4 * depth, LANES), F32),
             pltpu.VMEM((segments * owners * ROWS, LANES), F32),

time: 22.6 us -> 22 us (0.973)
  Pallas kernels: 7.62 us -> 7.03 us
    pallas_call x1, Pallas kernels: 6.83 us -> 6.23 us  [per_device(): pl.pallas_call(functools.partial(unet_kernel, owners), out_shape=(jax.Sha...]
where the time goes in v5:
time: 22 us; the launch traced here: 21.9 us
  blocking collectives  14.8 us (67%)
  Pallas kernels  7.03 us (32%)
    all_to_all x1, blocking collectives, per_device(): lax.all_to_all(slots, ('segment', 'patch'), split_axis=0, concat_axis=0,...  14.8 us
    pallas_call x1, Pallas kernels, per_device(): pl.pallas_call(functools.partial(unet_kernel, owners), out_shape=(jax.Sha...  6.23 us
    pallas_call x1, Pallas kernels, per_device(): pl.pallas_call(blend_kernel, out_shape=jax.ShapeDtypeStruct((CH_DEV, kind...  0.8 us

profile of v5, /device:TPU:0, one launch (start us, length us, event | category | flops | bytes accessed | tf_op | source)
XLA Modules:
  0.0 21.9 jit_solution(7586075089169481253)
XLA Ops:
  0.0 6.2 %shard_map.145 = (bf16[32,16,128]{2,1,0:T(8,128)(2,1)S(1)}, bf16[128,512]{1,0:T(8,128)(2,1)S(1)}) custom-call(s32[32]{0:T(128)} %first_block_h.1, s32[32]{0:T(128)} %offset_h.1, bf16[4,28,12,4,128]{4,3,2,1,0:T(4,128)(2,1)} %bitcast.10, bf16[4,28,12,4,128]{4,3,2,1,0:T(4,128)(2,1)} %bitcast.11, bf16[9,28,28]{2,1,0:T(8,128)(2,1)} %w1.1, ...), custom_call_target="tpu_custom_call" | custom-call | tf_op jit(solution)/shard_map/pallas_call | solution.py:399
  6.2 14.8 %all_to_all.5.mine = bf16[32,16,128]{2,1,0:T(8,128)(2,1)S(1)} all-to-all(bf16[32,16,128]{2,1,0:T(8,128)(2,1)S(1)} %get-tuple-element.8), channel_id=1, replica_groups=mesh['segment'=4,'patch'=8] {'segment','patch'}, dimensions={0} | all-to-all | bytes 262144 | tf_op jit(solution)/shard_map/all_to_all | solution.py:465
  21.1 0.8 %shard_map.146 = f32[8,3,4,128]{3,2,1,0:T(4,128)} custom-call(bf16[128,512]{1,0:T(8,128)(2,1)S(1)} %get-tuple-element.7.adder, bf16[32,16,128]{2,1,0:T(8,128)(2,1)S(1)} %all_to_all.5.mine), custom_call_target="tpu_custom_call" | custom-call | tf_op jit(solution)/shard_map/pallas_call | solution.py:466

commit v6 on v5

--- a/solution.py
+++ b/solution.py
@@ -98,7 +98,7 @@
 
 def column(row_ref, pad, rows, pick):
     pad[...] = jnp.zeros(pad.shape, F32)
-    pad[0:1, 0 : row_ref.shape[1]] = row_ref[...]
+    pad[0:1, 0 : row_ref.shape[1]] = row_ref[...].astype(F32)
     spread = jnp.broadcast_to(pad[0:1, :], (rows, LANES))
     want = pick(lax.broadcasted_iota(jnp.int32, (rows, LANES), 0))
     return jnp.sum(jnp.where(lane_index(rows) == want, spread, 0.0), axis=1, keepdims=True)
@@ -106,8 +106,10 @@
 
 def unet_kernel(
     owners,
+    depth,
     first_block_h,
     offset_h,
+    firsts_h,
     features,
     deep,
     w1,
@@ -125,6 +127,7 @@
     adder,
     first_block,
     offset,
+    firsts_v,
     feat_v,
     deep_v,
     w1_v,
@@ -159,7 +162,7 @@
     canvas,
     sems,
 ):
-    chans, along, depth = feat_v.shape[0], feat_v.shape[1], feat_v.shape[2]
+    chans, along, depth = feat_v.shape[0], feat_v.shape[1] // depth, depth
     plane = depth * SLOT
     me = lax.axis_index("segment")
     patch = lax.axis_index("patch") * features.shape[0] + me
@@ -183,6 +186,7 @@
                 (wy_h, wy),
                 (first_block_h, first_block),
                 (offset_h, offset),
+                (firsts_h, firsts_v),
             ]
         )
     ]
@@ -207,8 +211,7 @@
 
     def spread_cells(source):
         for c in range(chans):
-            for a in range(along):
-                cells[pl.ds((c * along + a) * depth, depth), :] = source[c, a].astype(F32)
+            cells[pl.ds(c * along * depth, along * depth), :] = source[c].astype(F32)
 
     def gathered(z, a):
         return cells[pl.ds(a * depth + z, SLOT, stride=along * depth), :]
@@ -216,22 +219,18 @@
     def own(r):
         return r
 
-    def make_adder():
+    def make_adder(block, firsts):
+        patches = firsts.shape[0]
+        each = LANES // ROWS
+        src = block * each + lane_index(patches) // ROWS
+        sender = (src % owners) * features.shape[0] + src // owners
+        mine = lax.broadcasted_iota(jnp.int32, (patches, LANES), 0) == sender
+        first = jnp.sum(jnp.where(mine, firsts, 0.0), axis=0, keepdims=True).astype(jnp.int32)
         row = lax.broadcasted_iota(jnp.int32, (adder.shape[0], LANES), 0)
         lane = lane_index(adder.shape[0])
-        here = lax.axis_index("patch")
-        each = LANES // ROWS
-        for block in range(adder.shape[1] // LANES):
-            index = jnp.full((1, LANES), -1, jnp.int32)
-            thin = lax.broadcasted_iota(jnp.int32, (1, LANES), 1)
-            for j in range(each):
-                src = block * each + j
-                first = first_block[(src % owners) * features.shape[0] + src // owners]
-                ahead = lax.rem(here - first + owners * CH_DEV, owners)
-                found = jnp.where(ahead < KMAX, (first + ahead) // owners, -1)
-                index = jnp.where(thin // ROWS == j, found, index)
-            keep = (row // ROWS == index) & (row % ROWS == lane % ROWS)
-            adder[:, block * LANES : (block + 1) * LANES] = jnp.where(keep, 1.0, 0.0).astype(BF)
+        ahead = (row // ROWS) * owners + lax.axis_index("patch") - first
+        keep = (ahead >= 0) & (ahead < KMAX) & (row % ROWS == lane % ROWS)
+        adder[:, block * LANES : (block + 1) * LANES] = jnp.where(keep, 1.0, 0.0).astype(BF)
 
     copies[0].wait()
     spread_cells(feat_v)
@@ -244,9 +243,7 @@
     build_first(p1, m1)
     for c in copies[2:]:
         c.wait()
-    make_adder()
-    for weight, padded in ((w2_v, p2), (w3_v, p3), (w4_v, p4)):
-        pad_taps(weight, padded)
+    pad_taps(w2_v, p2)
 
     def bias_rows(ref, copies_of):
         col = column(ref, pad, SLOT, own)
@@ -266,7 +263,7 @@
     bias = bias_rows(b1, GROUP)
     bias2, bias3, bias4 = (bias_rows(b, depth) for b in (b2, b3, b4))
     tasks = matrix_tasks(p2, 0, False, m2)
-    columns = [(z, group) for z in range(depth) for group in range(along // GROUP)]
+    columns = [(z, group) for group in range(along // GROUP) for z in range(depth)]
 
     def first_window(z, group):
         low = z * high + group * GROUP * SLOT
@@ -314,10 +311,12 @@
         for z in range(depth):
             put_shifted(xd, (a + 1) * plane + z * SLOT, gathered(z, a))
 
+    pad_taps(w3_v, p3)
     spread_cells(deep_v)
     tasks = matrix_tasks(p3, 0, True, m3s) + matrix_tasks(p3, chans, True, m3d)
     tasks += [functools.partial(deep_rows, a) for a in range(along)]
     layer([m2], [x1], bias2, x2, tasks)
+    pad_taps(w4_v, p4)
     tasks = matrix_tasks(p4, 0, True, m4t) + matrix_tasks(p4, chans, True, m4f)
     layer([m3s, m3d], [x2, xd], bias3, x3, tasks)
     bias = bias4
@@ -335,22 +334,26 @@
     across = jnp.broadcast_to(wy[...], (4 * depth, LANES))
     start = first_block[patch]
     move = offset[patch]
+    base = lax.rem(start, owners)
+    firsts = column(firsts_v, pad, firsts_v.shape[1], own)
+    tasks = [functools.partial(make_adder, b, firsts) for b in range(adder.shape[1] // LANES)]
     for a in range(0, along, 2):
         fourth = conv([m4t, m4f], [x3, x1], bias, a).astype(BF)
         logits = jnp.dot(head_b, fourth, preferred_element_type=F32) + head_bias
+        run(tasks, a // 2, along // 2)
         value = jax.nn.sigmoid(logits)
         for h in range(2):
             part = value[:, h * LANES : (h + 1) * LANES] * (
                 blend_z * float(sa[a + h]) * across
             )
             place = move + (a + h)
-            owner = lax.rem(start + place // CW, owners)
-            cell = lax.rem(place, CW)
+            owner = base + lax.div(place, CW)
+            owner = jnp.where(owner >= owners, owner - owners, owner)
+            spot = owner * ROWS + lax.rem(place, CW)
             for z in range(depth):
                 for kind in range(kinds):
                     r = z * 4 + kind
-                    to = (z * owners + owner) * ROWS + kind * CW + cell
-                    canvas[pl.ds(to, 1), :] = part[r : r + 1, :]
+                    canvas[pl.ds(spot + (z * owners * ROWS + kind * CW), 1), :] = part[r : r + 1, :]
     for slot in range(out.shape[0]):
         out[slot] = canvas[slot * ROWS : (slot + 1) * ROWS, :].astype(BF)
 
@@ -389,26 +392,33 @@
     count, chans, depth, along, across = features.shape
     kinds = head_weight.shape[0]
     assert count == segments and depth == segments and across == LANES
+    assert block_first.shape[0] <= LANES and owners >= KMAX
     assert along % GROUP == 0 and kinds * CW <= ROWS and chans <= SLOT and depth * SLOT == LANES
     plane = depth * SLOT
+
+    def by_cell(values):
+        rows = (count, chans, along * depth, across)
+        return values.transpose(0, 1, 3, 2, 4).reshape(rows)
+
     vmem = pl.BlockSpec(memory_space=pltpu.VMEM)
     hbm = pl.BlockSpec(memory_space=pltpu.HBM)
     act = pltpu.VMEM((3, (along + 2) * plane, LANES), BF)
     taps = pltpu.VMEM((plane, 9 * LANES), BF)
     wy = jnp.asarray(bump(across)).reshape(1, across)
     slots, adder = pl.pallas_call(
-        functools.partial(unet_kernel, owners),
+        functools.partial(unet_kernel, owners, depth),
         out_shape=(
             jax.ShapeDtypeStruct((segments * owners, ROWS, across), BF),
             jax.ShapeDtypeStruct((CH_DEV * ROWS, segments * owners * ROWS), BF),
         ),
-        in_specs=[hbm] * 15,
+        in_specs=[hbm] * 16,
         out_specs=(vmem, vmem),
         scratch_shapes=[
             pltpu.SMEM(block_first.shape, jnp.int32),
             pltpu.SMEM(block_first.shape, jnp.int32),
-            pltpu.VMEM((chans, along, depth, across), BF),
-            pltpu.VMEM((chans, along, depth, across), BF),
+            pltpu.VMEM((1, block_first.shape[0]), jnp.int32),
+            pltpu.VMEM((chans, along * depth, across), BF),
+            pltpu.VMEM((chans, along * depth, across), BF),
             pltpu.VMEM(weight_first.shape, BF),
             pltpu.VMEM(weight_second.shape, BF),
             pltpu.VMEM(weight_third.shape, BF),
@@ -439,7 +449,7 @@
             pltpu.VMEM((8, LANES), F32),
             pltpu.VMEM((4 * depth, LANES), F32),
             pltpu.VMEM((segments * owners * ROWS, LANES), F32),
-            pltpu.SemaphoreType.DMA((15,)),
+            pltpu.SemaphoreType.DMA((16,)),
         ],
         compiler_params=pltpu.CompilerParams(vmem_limit_bytes=48 * 2**20),
     )(
@@ -447,8 +457,9 @@
             pltpu.HBM,
         block_first,
         block_offset,
-        features.transpose(0, 1, 3, 2, 4),
-        deep_path.transpose(0, 1, 3, 2, 4),
+        block_first.reshape(1, -1),
+        by_cell(features),
+        by_cell(deep_path),
         weight_first,
         weight_second,
         weight_third,

time: 22 us -> 21.9 us (level)
  no operation moved by 1% of the time
where the time goes in v6:
time: 21.9 us; the launch traced here: 21.7 us
  blocking collectives  14.8 us (68%)
  Pallas kernels  6.85 us (31%)
    all_to_all x1, blocking collectives, per_device(): lax.all_to_all(slots, ('segment', 'patch'), split_axis=0, concat_axis=0,...  14.8 us
    pallas_call x1, Pallas kernels, per_device(): pl.pallas_call(functools.partial(unet_kernel, owners, depth), out_shape=(...  6.05 us
    pallas_call x1, Pallas kernels, per_device(): pl.pallas_call(blend_kernel, out_shape=jax.ShapeDtypeStruct((CH_DEV, kind...  0.8 us

profile of v6, /device:TPU:0, one launch (start us, length us, event | category | flops | bytes accessed | tf_op | source)
XLA Modules:
  0.0 21.7 jit_solution(3104106472270584427)
XLA Ops:
  0.0 6.1 %shard_map.145 = (bf16[32,16,128]{2,1,0:T(8,128)(2,1)S(1)}, bf16[128,512]{1,0:T(8,128)(2,1)S(1)}) custom-call(s32[32]{0:T(128)} %first_block_h.1, s32[32]{0:T(128)} %offset_h.1, s32[1,32]{1,0:T(1,128)} %bitcast.17, bf16[4,28,48,128]{3,2,1,0:T(8,128)(2,1)} %bitcast.15, bf16[4,28,48,128]{3,2,1,0:T(8,128)(2,1)} %bitcast.16, bf16[9,28,28]{2,1,0:T(8,128)(2,1)} %w1.1, ...), custom_call_target="tpu_custom_call" | custom-call | tf_op jit(solution)/shard_map/pallas_call | solution.py:408
  6.1 14.8 %all_to_all.5.mine = bf16[32,16,128]{2,1,0:T(8,128)(2,1)S(1)} all-to-all(bf16[32,16,128]{2,1,0:T(8,128)(2,1)S(1)} %get-tuple-element.8), channel_id=1, replica_groups=mesh['segment'=4,'patch'=8] {'segment','patch'}, dimensions={0} | all-to-all | bytes 262144 | tf_op jit(solution)/shard_map/all_to_all | solution.py:476
  20.9 0.8 %shard_map.146 = f32[8,3,4,128]{3,2,1,0:T(4,128)} custom-call(bf16[128,512]{1,0:T(8,128)(2,1)S(1)} %get-tuple-element.7.adder, bf16[32,16,128]{2,1,0:T(8,128)(2,1)S(1)} %all_to_all.5.mine), custom_call_target="tpu_custom_call" | custom-call | tf_op jit(solution)/shard_map/pallas_call | solution.py:477

commit v7 on v6

--- a/solution.py
+++ b/solution.py
@@ -171,13 +171,13 @@
         pltpu.make_async_copy(src, dst, sems.at[i])
         for i, (src, dst) in enumerate(
             [
+                (w1, w1_v),
                 (features.at[me], feat_v),
-                (w1, w1_v),
                 (w2, w2_v),
+                (b1_h, b1),
+                (w3, w3_v),
                 (deep.at[me], deep_v),
-                (w3, w3_v),
                 (w4, w4_v),
-                (b1_h, b1),
                 (b2_h, b2),
                 (b3_h, b3),
                 (b4_h, b4),
@@ -206,15 +206,16 @@
         padded[...] = jnp.zeros(padded.shape, BF)
     head[...] = jnp.zeros(head.shape, F32)
     canvas[...] = jnp.zeros(canvas.shape, F32)
-    used = chans * along * depth
+    pitch = cells.shape[0] // SLOT
+    used = chans * pitch
     cells[used:, :] = jnp.zeros((cells.shape[0] - used, LANES), F32)
 
     def spread_cells(source):
         for c in range(chans):
-            cells[pl.ds(c * along * depth, along * depth), :] = source[c].astype(F32)
+            cells[pl.ds(c * pitch, along * depth), :] = source[c].astype(F32)
 
     def gathered(z, a):
-        return cells[pl.ds(a * depth + z, SLOT, stride=along * depth), :]
+        return cells[pl.ds(a * depth + z, SLOT, stride=pitch), :]
 
     def own(r):
         return r
@@ -232,37 +233,35 @@
         keep = (ahead >= 0) & (ahead < KMAX) & (row % ROWS == lane % ROWS)
         adder[:, block * LANES : (block + 1) * LANES] = jnp.where(keep, 1.0, 0.0).astype(BF)
 
-    copies[0].wait()
-    spread_cells(feat_v)
-    for z in range(depth):
-        for a in range(along):
-            put_shifted(xf, z * high + (a + 1) * SLOT, gathered(z, a))
-
-    copies[1].wait()
-    pad_taps(w1_v, p1)
-    build_first(p1, m1)
-    for c in copies[2:]:
-        c.wait()
-    pad_taps(w2_v, p2)
-
-    def bias_rows(ref, copies_of):
-        col = column(ref, pad, SLOT, own)
-        tile = jnp.broadcast_to(col, (SLOT, LANES))
-        return jnp.concatenate([tile] * copies_of, axis=0)
-
     def matrix_tasks(padded, low, wide, big):
         return [
             functools.partial(build_bands, padded, low, chans, wide, big, depth, da)
             for da in range(3)
         ]
 
+    for c in copies[0:2]:
+        c.wait()
+    pad_taps(w1_v, p1)
+    build_first(p1, m1)
+    spread_cells(feat_v)
+    for z in range(depth):
+        for a in range(along):
+            put_shifted(xf, z * high + (a + 1) * SLOT, gathered(z, a))
+
+    for c in copies[2:]:
+        c.wait()
+    def bias_rows(ref, copies_of):
+        col = column(ref, pad, SLOT, own)
+        tile = jnp.broadcast_to(col, (SLOT, LANES))
+        return jnp.concatenate([tile] * copies_of, axis=0)
+
     def run(tasks, step, steps):
         for task in tasks[len(tasks) * step // steps : len(tasks) * (step + 1) // steps]:
             task()
 
     bias = bias_rows(b1, GROUP)
     bias2, bias3, bias4 = (bias_rows(b, depth) for b in (b2, b3, b4))
-    tasks = matrix_tasks(p2, 0, False, m2)
+    tasks = [functools.partial(pad_taps, w2_v, p2)] + matrix_tasks(p2, 0, False, m2) + [functools.partial(pad_taps, w3_v, p3)]
     columns = [(z, group) for group in range(along // GROUP) for z in range(depth)]
 
     def first_window(z, group):
@@ -311,10 +310,7 @@
         for z in range(depth):
             put_shifted(xd, (a + 1) * plane + z * SLOT, gathered(z, a))
 
-    pad_taps(w3_v, p3)
-    spread_cells(deep_v)
-    tasks = matrix_tasks(p3, 0, True, m3s) + matrix_tasks(p3, chans, True, m3d)
-    tasks += [functools.partial(deep_rows, a) for a in range(along)]
+    tasks = matrix_tasks(p3, 0, True, m3s) + matrix_tasks(p3, chans, True, m3d) + [functools.partial(spread_cells, deep_v)] + [functools.partial(deep_rows, a) for a in range(along)]
     layer([m2], [x1], bias2, x2, tasks)
     pad_taps(w4_v, p4)
     tasks = matrix_tasks(p4, 0, True, m4t) + matrix_tasks(p4, chans, True, m4f)
@@ -430,7 +426,7 @@
             pltpu.VMEM(head_weight.shape, BF),
             pltpu.VMEM((1, kinds), F32),
             pltpu.VMEM((1, across), F32),
-            pltpu.VMEM((SLOT * along * depth, LANES), F32),
+            pltpu.VMEM((SLOT * (along * depth + 1), LANES), F32),
             pltpu.VMEM((3, depth * (along + 2) * SLOT, LANES), BF),
             act,
             act,

time: 21.9 us -> 21.6 us (0.986)
  Pallas kernels: 6.85 us -> 6.57 us
    pallas_call x1, Pallas kernels: 6.05 us -> 5.77 us  [per_device(): pl.pallas_call(functools.partial(unet_kernel, owners, depth), out_shape=(...]
where the time goes in v7:
time: 21.6 us; the launch traced here: 21.4 us
  blocking collectives  14.8 us (69%)
  Pallas kernels  6.57 us (30%)
    all_to_all x1, blocking collectives, per_device(): lax.all_to_all(slots, ('segment', 'patch'), split_axis=0, concat_axis=0,...  14.8 us
    pallas_call x1, Pallas kernels, per_device(): pl.pallas_call(functools.partial(unet_kernel, owners, depth), out_shape=(...  5.77 us
    pallas_call x1, Pallas kernels, per_device(): pl.pallas_call(blend_kernel, out_shape=jax.ShapeDtypeStruct((CH_DEV, kind...  0.8 us

profile of v7, /device:TPU:0, one launch (start us, length us, event | category | flops | bytes accessed | tf_op | source)
XLA Modules:
  0.0 21.4 jit_solution(2089011318743521697)
XLA Ops:
  0.0 5.8 %shard_map.145 = (bf16[32,16,128]{2,1,0:T(8,128)(2,1)S(1)}, bf16[128,512]{1,0:T(8,128)(2,1)S(1)}) custom-call(s32[32]{0:T(128)} %first_block_h.1, s32[32]{0:T(128)} %offset_h.1, s32[1,32]{1,0:T(1,128)} %bitcast.17, bf16[4,28,48,128]{3,2,1,0:T(8,128)(2,1)} %bitcast.15, bf16[4,28,48,128]{3,2,1,0:T(8,128)(2,1)} %bitcast.16, bf16[9,28,28]{2,1,0:T(8,128)(2,1)} %w1.1, ...), custom_call_target="tpu_custom_call" | custom-call | tf_op jit(solution)/shard_map/pallas_call | solution.py:404
  5.8 14.8 %all_to_all.5.mine = bf16[32,16,128]{2,1,0:T(8,128)(2,1)S(1)} all-to-all(bf16[32,16,128]{2,1,0:T(8,128)(2,1)S(1)} %get-tuple-element.8), channel_id=1, replica_groups=mesh['segment'=4,'patch'=8] {'segment','patch'}, dimensions={0} | all-to-all | bytes 262144 | tf_op jit(solution)/shard_map/all_to_all | solution.py:472
  20.6 0.8 %shard_map.146 = f32[8,3,4,128]{3,2,1,0:T(4,128)} custom-call(bf16[128,512]{1,0:T(8,128)(2,1)S(1)} %get-tuple-element.7.adder, bf16[32,16,128]{2,1,0:T(8,128)(2,1)S(1)} %all_to_all.5.mine), custom_call_target="tpu_custom_call" | custom-call | tf_op jit(solution)/shard_map/pallas_call | solution.py:473

commit v8 on v7

--- a/solution.py
+++ b/solution.py
@@ -60,25 +60,31 @@
         padded[t, 0:rows, 0:cols] = weight[t]
 
 
-def build_bands(padded, low, chans, wide, big, depth, da):
+def build_bases(padded, low, chans, wide, bases, place, da):
     parts = []
     for dz in range(3):
         taps = padded[9 * dz + 3 * da : 9 * dz + 3 * da + 3].reshape(3 * SLOT, LANES)
         if low or wide:
             taps = masked(taps, lane_mask(low, low + chans))
-        parts.append(turned(taps, dz * SLOT - low))
-    base = parts[0] + parts[1] + parts[2]
-    for z in range(depth):
-        moved = turned(base, (z - 1) * SLOT)
-        if z == 0:
-            moved = masked(moved, lane_mask(0, LANES - SLOT))
-        if z == depth - 1:
-            moved = masked(moved, lane_mask(SLOT, LANES))
-        for dy in range(3):
-            k = da * 3 + dy
-            big[z * SLOT : (z + 1) * SLOT, k * LANES : (k + 1) * LANES] = moved[
-                dy * SLOT : (dy + 1) * SLOT
-            ]
+        parts.append(turned(taps, dz * chans - low))
+    first = (place + 3 * da) * SLOT
+    bases[first : first + 3 * SLOT, :] = parts[0] + parts[1] + parts[2]
+
+
+def build_rows(bases, blocks, chans, big, depth, z):
+    dense = depth * chans
+    columns = {}
+    for k in range(blocks):
+        moved = turned(bases[k * SLOT : (k + 1) * SLOT, :], k * dense + (z - 1) * chans)
+        low = k * dense + max(z - 1, 0) * chans
+        high = k * dense + min(z + 2, depth) * chans
+        for j in range(low // LANES, (high - 1) // LANES + 1):
+            tile = lane_mask(max(low - j * LANES, 0), min(high - j * LANES, LANES))
+            piece = masked(moved, tile)
+            columns[j] = columns[j] + piece if j in columns else piece
+    for j, value in columns.items():
+        lanes = min(LANES, blocks * dense - j * LANES)
+        big[z * chans : (z + 1) * chans, j * LANES : j * LANES + lanes] = value[:chans, :lanes]
 
 
 def build_first(padded, big):
@@ -149,10 +155,11 @@
     x3,
     m1,
     m2,
-    m3s,
-    m3d,
-    m4t,
-    m4f,
+    m3,
+    m4,
+    q2,
+    q3,
+    q4,
     p1,
     p2,
     p3,
@@ -163,7 +170,7 @@
     sems,
 ):
     chans, along, depth = feat_v.shape[0], feat_v.shape[1] // depth, depth
-    plane = depth * SLOT
+    dense = depth * chans
     me = lax.axis_index("segment")
     patch = lax.axis_index("patch") * features.shape[0] + me
 
@@ -195,8 +202,8 @@
 
     for act in (x1, x2, xd, x3):
         for dy in range(3):
-            act[dy, 0:plane, :] = jnp.zeros((plane, LANES), BF)
-            act[dy, (along + 1) * plane : (along + 2) * plane, :] = jnp.zeros((plane, LANES), BF)
+            act[dy, 0:dense, :] = jnp.zeros((dense, LANES), BF)
+            act[dy, (along + 1) * dense : (along + 2) * dense, :] = jnp.zeros((dense, LANES), BF)
     high = (along + 2) * SLOT
     for dy in range(3):
         for z in range(depth):
@@ -233,10 +240,18 @@
         keep = (ahead >= 0) & (ahead < KMAX) & (row % ROWS == lane % ROWS)
         adder[:, block * LANES : (block + 1) * LANES] = jnp.where(keep, 1.0, 0.0).astype(BF)
 
-    def matrix_tasks(padded, low, wide, big):
-        return [
-            functools.partial(build_bands, padded, low, chans, wide, big, depth, da)
+    def matrix_tasks(padded, bases, big):
+        sources = big.shape[1] // (9 * dense)
+        tasks = [
+            functools.partial(
+                build_bases, padded, i * chans, chans, sources > 1, bases, 9 * i, da
+            )
+            for i in range(sources)
             for da in range(3)
+        ]
+        return tasks + [
+            functools.partial(build_rows, bases, 9 * sources, chans, big, depth, z)
+            for z in range(depth)
         ]
 
     for c in copies[0:2]:
@@ -250,18 +265,16 @@
 
     for c in copies[2:]:
         c.wait()
-    def bias_rows(ref, copies_of):
-        col = column(ref, pad, SLOT, own)
-        tile = jnp.broadcast_to(col, (SLOT, LANES))
-        return jnp.concatenate([tile] * copies_of, axis=0)
+    def bias_rows(ref, rows, each):
+        return jnp.broadcast_to(column(ref, pad, rows, lambda r: r % each), (rows, LANES))
 
     def run(tasks, step, steps):
         for task in tasks[len(tasks) * step // steps : len(tasks) * (step + 1) // steps]:
             task()
 
-    bias = bias_rows(b1, GROUP)
-    bias2, bias3, bias4 = (bias_rows(b, depth) for b in (b2, b3, b4))
-    tasks = [functools.partial(pad_taps, w2_v, p2)] + matrix_tasks(p2, 0, False, m2) + [functools.partial(pad_taps, w3_v, p3)]
+    bias = bias_rows(b1, GROUP * SLOT, SLOT)
+    bias2, bias3, bias4 = (bias_rows(b, dense, chans) for b in (b2, b3, b4))
+    tasks = [functools.partial(pad_taps, w2_v, p2)] + matrix_tasks(p2, q2, m2) + [functools.partial(pad_taps, w3_v, p3)]
     columns = [(z, group) for group in range(along // GROUP) for z in range(depth)]
 
     def first_window(z, group):
@@ -270,57 +283,61 @@
         pieces += [xf[dy, pl.ds(low + LANES, LANES // 2), :] for dy in range(3)]
         return jnp.concatenate(pieces, axis=0)
 
+    sections = []
     for pair in range(0, len(columns), 2):
         rhs = jnp.concatenate([first_window(*c) for c in columns[pair : pair + 2]], axis=1)
         got = jnp.dot(m1[:, 0 : rhs.shape[0]], rhs, preferred_element_type=F32)
         run(tasks, pair // 2, len(columns) // 2)
         for h, (z, group) in enumerate(columns[pair : pair + 2]):
-            part = jnp.maximum(got[:, h * LANES : (h + 1) * LANES] + bias, 0.0)
+            sections.append(jnp.maximum(got[:, h * LANES : (h + 1) * LANES] + bias, 0.0))
+            if len(sections) < depth:
+                continue
             for a in range(GROUP):
+                low = a * SLOT
                 put_shifted(
                     x1,
-                    (1 + group * GROUP + a) * plane + z * SLOT,
-                    part[a * SLOT : (a + 1) * SLOT],
+                    (1 + group * GROUP + a) * dense,
+                    jnp.concatenate([part[low : low + chans] for part in sections], axis=0),
                 )
+            sections = []
 
     def window_of(act, a):
         return jnp.concatenate(
-            [act[dy, pl.ds((a + da) * plane, plane), :] for da in range(3) for dy in range(3)],
+            [act[dy, pl.ds((a + da) * dense, dense), :] for da in range(3) for dy in range(3)],
             axis=0,
         )
 
-    def conv(mats, acts, bias, a):
-        matrix = jnp.concatenate([m[...] for m in mats], axis=1) if len(mats) > 1 else mats[0][...]
+    def conv(matrix, acts, bias, a):
         cols = []
         for b in (a, a + 1):
             parts = [window_of(x, b) for x in acts]
             cols.append(jnp.concatenate(parts, axis=0) if len(parts) > 1 else parts[0])
-        got = jnp.dot(matrix, jnp.concatenate(cols, axis=1), preferred_element_type=F32)
+        got = jnp.dot(matrix[...], jnp.concatenate(cols, axis=1), preferred_element_type=F32)
         wide = jnp.concatenate([bias, bias], axis=1)
         return jnp.maximum(got + wide, 0.0)
 
-    def layer(mats, acts, bias, result, tasks):
+    def layer(matrix, acts, bias, result, tasks):
         for a in range(0, along, 2):
-            got = conv(mats, acts, bias, a)
+            got = conv(matrix, acts, bias, a)
             run(tasks, a // 2, along // 2)
             for h in range(2):
-                put_shifted(result, (1 + a + h) * plane, got[:, h * LANES : (h + 1) * LANES])
+                put_shifted(result, (1 + a + h) * dense, got[:, h * LANES : (h + 1) * LANES])
 
     def deep_rows(a):
-        for z in range(depth):
-            put_shifted(xd, (a + 1) * plane + z * SLOT, gathered(z, a))
-
-    tasks = matrix_tasks(p3, 0, True, m3s) + matrix_tasks(p3, chans, True, m3d) + [functools.partial(spread_cells, deep_v)] + [functools.partial(deep_rows, a) for a in range(along)]
-    layer([m2], [x1], bias2, x2, tasks)
+        value = jnp.concatenate([gathered(z, a)[:chans] for z in range(depth)], axis=0)
+        put_shifted(xd, (a + 1) * dense, value)
+
+    tasks = matrix_tasks(p3, q3, m3) + [functools.partial(spread_cells, deep_v)] + [functools.partial(deep_rows, a) for a in range(along)]
+    layer(m2, [x1], bias2, x2, tasks)
     pad_taps(w4_v, p4)
-    tasks = matrix_tasks(p4, 0, True, m4t) + matrix_tasks(p4, chans, True, m4f)
-    layer([m3s, m3d], [x2, xd], bias3, x3, tasks)
+    tasks = matrix_tasks(p4, q4, m4)
+    layer(m3, [x2, xd], bias3, x3, tasks)
     bias = bias4
     kinds = hw.shape[0]
     tap = hw[...].astype(F32)
     for z in range(depth):
-        head[z * 4 : z * 4 + kinds, z * SLOT : z * SLOT + chans] = tap
-    head_b = head[...].astype(BF)
+        head[z * 4 : z * 4 + kinds, z * chans : (z + 1) * chans] = tap
+    head_b = head[:, 0:dense].astype(BF)
     head_bias = column(hb, pad, 4 * depth, lambda r: r % 4)
     sz, sa = bump(depth), bump(along)
     row = lax.broadcasted_iota(jnp.int32, (4 * depth, LANES), 0)
@@ -334,7 +351,7 @@
     firsts = column(firsts_v, pad, firsts_v.shape[1], own)
     tasks = [functools.partial(make_adder, b, firsts) for b in range(adder.shape[1] // LANES)]
     for a in range(0, along, 2):
-        fourth = conv([m4t, m4f], [x3, x1], bias, a).astype(BF)
+        fourth = conv(m4, [x3, x1], bias, a).astype(BF)
         logits = jnp.dot(head_b, fourth, preferred_element_type=F32) + head_bias
         run(tasks, a // 2, along // 2)
         value = jax.nn.sigmoid(logits)
@@ -390,7 +407,8 @@
     assert count == segments and depth == segments and across == LANES
     assert block_first.shape[0] <= LANES and owners >= KMAX
     assert along % GROUP == 0 and kinds * CW <= ROWS and chans <= SLOT and depth * SLOT == LANES
-    plane = depth * SLOT
+    dense = depth * chans
+    assert dense % TILE == 0
 
     def by_cell(values):
         rows = (count, chans, along * depth, across)
@@ -398,8 +416,9 @@
 
     vmem = pl.BlockSpec(memory_space=pltpu.VMEM)
     hbm = pl.BlockSpec(memory_space=pltpu.HBM)
-    act = pltpu.VMEM((3, (along + 2) * plane, LANES), BF)
-    taps = pltpu.VMEM((plane, 9 * LANES), BF)
+    act = pltpu.VMEM((3, (along + 2) * dense, LANES), BF)
+    one = pltpu.VMEM((dense, 9 * dense), BF)
+    two = pltpu.VMEM((dense, 18 * dense), BF)
     wy = jnp.asarray(bump(across)).reshape(1, across)
     slots, adder = pl.pallas_call(
         functools.partial(unet_kernel, owners, depth),
@@ -433,11 +452,12 @@
             act,
             act,
             pltpu.VMEM((GROUP * SLOT, 5 * LANES), BF),
-            taps,
-            taps,
-            taps,
-            taps,
-            taps,
+            one,
+            two,
+            two,
+            pltpu.VMEM((9 * SLOT, LANES), BF),
+            pltpu.VMEM((18 * SLOT, LANES), BF),
+            pltpu.VMEM((18 * SLOT, LANES), BF),
             pltpu.VMEM((9, SLOT, LANES), BF),
             pltpu.VMEM((27, SLOT, LANES), BF),
             pltpu.VMEM((27, SLOT, LANES), BF),

time: 21.6 us -> 21.3 us (0.986)
  Pallas kernels: 6.57 us -> 6.29 us
    pallas_call x1, Pallas kernels: 5.77 us -> 5.49 us  [per_device(): pl.pallas_call(functools.partial(unet_kernel, owners, depth), out_shape=(...]
where the time goes in v8:
time: 21.3 us; the launch traced here: 21.1 us
  blocking collectives  14.8 us (69%)
  Pallas kernels  6.29 us (30%)
    all_to_all x1, blocking collectives, per_device(): lax.all_to_all(slots, ('segment', 'patch'), split_axis=0, concat_axis=0,...  14.8 us
    pallas_call x1, Pallas kernels, per_device(): pl.pallas_call(functools.partial(unet_kernel, owners, depth), out_shape=(...  5.49 us
    pallas_call x1, Pallas kernels, per_device(): pl.pallas_call(blend_kernel, out_shape=jax.ShapeDtypeStruct((CH_DEV, kind...  0.8 us

profile of v8, /device:TPU:0, one launch (start us, length us, event | category | flops | bytes accessed | tf_op | source)
XLA Modules:
  0.0 21.1 jit_solution(513010526722845330)
XLA Ops:
  0.0 5.5 %shard_map.145 = (bf16[32,16,128]{2,1,0:T(8,128)(2,1)S(1)}, bf16[128,512]{1,0:T(8,128)(2,1)S(1)}) custom-call(s32[32]{0:T(128)} %first_block_h.1, s32[32]{0:T(128)} %offset_h.1, s32[1,32]{1,0:T(1,128)} %bitcast.17, bf16[4,28,48,128]{3,2,1,0:T(8,128)(2,1)} %bitcast.15, bf16[4,28,48,128]{3,2,1,0:T(8,128)(2,1)} %bitcast.16, bf16[9,28,28]{2,1,0:T(8,128)(2,1)} %w1.1, ...), custom_call_target="tpu_custom_call" | custom-call | tf_op jit(solution)/shard_map/pallas_call | solution.py:423
  5.5 14.8 %all_to_all.5.mine = bf16[32,16,128]{2,1,0:T(8,128)(2,1)S(1)} all-to-all(bf16[32,16,128]{2,1,0:T(8,128)(2,1)S(1)} %get-tuple-element.8), channel_id=1, replica_groups=mesh['segment'=4,'patch'=8] {'segment','patch'}, dimensions={0} | all-to-all | bytes 262144 | tf_op jit(solution)/shard_map/all_to_all | solution.py:492
  20.3 0.8 %shard_map.146 = f32[8,3,4,128]{3,2,1,0:T(4,128)} custom-call(bf16[128,512]{1,0:T(8,128)(2,1)S(1)} %get-tuple-element.7.adder, bf16[32,16,128]{2,1,0:T(8,128)(2,1)S(1)} %all_to_all.5.mine), custom_call_target="tpu_custom_call" | custom-call | tf_op jit(solution)/shard_map/pallas_call | solution.py:493

commit v9 on v8

--- a/solution.py
+++ b/solution.py
@@ -16,6 +16,7 @@
 SLOT = 32
 TILE = 16
 ROWS = 16
+WIDE = 4
 GROUP = 4
 BF = jnp.bfloat16
 F32 = jnp.float32
@@ -309,18 +310,18 @@
 
     def conv(matrix, acts, bias, a):
         cols = []
-        for b in (a, a + 1):
+        for b in range(a, a + WIDE):
             parts = [window_of(x, b) for x in acts]
             cols.append(jnp.concatenate(parts, axis=0) if len(parts) > 1 else parts[0])
         got = jnp.dot(matrix[...], jnp.concatenate(cols, axis=1), preferred_element_type=F32)
-        wide = jnp.concatenate([bias, bias], axis=1)
+        wide = jnp.concatenate([bias] * WIDE, axis=1)
         return jnp.maximum(got + wide, 0.0)
 
     def layer(matrix, acts, bias, result, tasks):
-        for a in range(0, along, 2):
+        for a in range(0, along, WIDE):
             got = conv(matrix, acts, bias, a)
-            run(tasks, a // 2, along // 2)
-            for h in range(2):
+            run(tasks, a // WIDE, along // WIDE)
+            for h in range(WIDE):
                 put_shifted(result, (1 + a + h) * dense, got[:, h * LANES : (h + 1) * LANES])
 
     def deep_rows(a):
@@ -350,12 +351,12 @@
     base = lax.rem(start, owners)
     firsts = column(firsts_v, pad, firsts_v.shape[1], own)
     tasks = [functools.partial(make_adder, b, firsts) for b in range(adder.shape[1] // LANES)]
-    for a in range(0, along, 2):
+    for a in range(0, along, WIDE):
         fourth = conv(m4, [x3, x1], bias, a).astype(BF)
         logits = jnp.dot(head_b, fourth, preferred_element_type=F32) + head_bias
-        run(tasks, a // 2, along // 2)
+        run(tasks, a // WIDE, along // WIDE)
         value = jax.nn.sigmoid(logits)
-        for h in range(2):
+        for h in range(WIDE):
             part = value[:, h * LANES : (h + 1) * LANES] * (
                 blend_z * float(sa[a + h]) * across
             )

time: 21.3 us -> 20.9 us (0.981)
  Pallas kernels: 6.29 us -> 5.85 us
    pallas_call x1, Pallas kernels: 5.49 us -> 5.05 us  [per_device(): pl.pallas_call(functools.partial(unet_kernel, owners, depth), out_shape=(...]
where the time goes in v9:
time: 20.9 us; the launch traced here: 20.7 us
  blocking collectives  14.8 us (71%)
  Pallas kernels  5.85 us (28%)
    all_to_all x1, blocking collectives, per_device(): lax.all_to_all(slots, ('segment', 'patch'), split_axis=0, concat_axis=0,...  14.8 us
    pallas_call x1, Pallas kernels, per_device(): pl.pallas_call(functools.partial(unet_kernel, owners, depth), out_shape=(...  5.05 us
    pallas_call x1, Pallas kernels, per_device(): pl.pallas_call(blend_kernel, out_shape=jax.ShapeDtypeStruct((CH_DEV, kind...  0.8 us

profile of v9, /device:TPU:0, one launch (start us, length us, event | category | flops | bytes accessed | tf_op | source)
XLA Modules:
  0.0 20.7 jit_solution(10158596871157071780)
XLA Ops:
  0.0 5.1 %shard_map.145 = (bf16[32,16,128]{2,1,0:T(8,128)(2,1)S(1)}, bf16[128,512]{1,0:T(8,128)(2,1)S(1)}) custom-call(s32[32]{0:T(128)} %first_block_h.1, s32[32]{0:T(128)} %offset_h.1, s32[1,32]{1,0:T(1,128)} %bitcast.17, bf16[4,28,48,128]{3,2,1,0:T(8,128)(2,1)} %bitcast.15, bf16[4,28,48,128]{3,2,1,0:T(8,128)(2,1)} %bitcast.16, bf16[9,28,28]{2,1,0:T(8,128)(2,1)} %w1.1, ...), custom_call_target="tpu_custom_call" | custom-call | tf_op jit(solution)/shard_map/pallas_call | solution.py:424
  5.1 14.8 %all_to_all.5.mine = bf16[32,16,128]{2,1,0:T(8,128)(2,1)S(1)} all-to-all(bf16[32,16,128]{2,1,0:T(8,128)(2,1)S(1)} %get-tuple-element.8), channel_id=1, replica_groups=mesh['segment'=4,'patch'=8] {'segment','patch'}, dimensions={0} | all-to-all | bytes 262144 | tf_op jit(solution)/shard_map/all_to_all | solution.py:493
  19.9 0.8 %shard_map.146 = f32[8,3,4,128]{3,2,1,0:T(4,128)} custom-call(bf16[128,512]{1,0:T(8,128)(2,1)S(1)} %get-tuple-element.7.adder, bf16[32,16,128]{2,1,0:T(8,128)(2,1)S(1)} %all_to_all.5.mine), custom_call_target="tpu_custom_call" | custom-call | tf_op jit(solution)/shard_map/pallas_call | solution.py:494

commit v10 on v9

--- a/solution.py
+++ b/solution.py
@@ -285,11 +285,11 @@
         return jnp.concatenate(pieces, axis=0)
 
     sections = []
-    for pair in range(0, len(columns), 2):
-        rhs = jnp.concatenate([first_window(*c) for c in columns[pair : pair + 2]], axis=1)
+    for pair in range(0, len(columns), depth):
+        rhs = jnp.concatenate([first_window(*c) for c in columns[pair : pair + depth]], axis=1)
         got = jnp.dot(m1[:, 0 : rhs.shape[0]], rhs, preferred_element_type=F32)
-        run(tasks, pair // 2, len(columns) // 2)
-        for h, (z, group) in enumerate(columns[pair : pair + 2]):
+        run(tasks, pair // depth, len(columns) // depth)
+        for h, (z, group) in enumerate(columns[pair : pair + depth]):
             sections.append(jnp.maximum(got[:, h * LANES : (h + 1) * LANES] + bias, 0.0))
             if len(sections) < depth:
                 continue

time: 20.9 us -> 20.9 us (level)
  no operation moved by 1% of the time
where the time goes in v10:
time: 20.9 us; the launch traced here: 20.7 us
  blocking collectives  14.9 us (71%)
  Pallas kernels  5.83 us (28%)
    all_to_all x1, blocking collectives, per_device(): lax.all_to_all(slots, ('segment', 'patch'), split_axis=0, concat_axis=0,...  14.9 us
    pallas_call x1, Pallas kernels, per_device(): pl.pallas_call(functools.partial(unet_kernel, owners, depth), out_shape=(...  5.03 us
    pallas_call x1, Pallas kernels, per_device(): pl.pallas_call(blend_kernel, out_shape=jax.ShapeDtypeStruct((CH_DEV, kind...  0.8 us

profile of v10, /device:TPU:0, one launch (start us, length us, event | category | flops | bytes accessed | tf_op | source)
XLA Modules:
  0.0 20.7 jit_solution(10584249921266608192)
XLA Ops:
  0.0 5.0 %shard_map.145 = (bf16[32,16,128]{2,1,0:T(8,128)(2,1)S(1)}, bf16[128,512]{1,0:T(8,128)(2,1)S(1)}) custom-call(s32[32]{0:T(128)} %first_block_h.1, s32[32]{0:T(128)} %offset_h.1, s32[1,32]{1,0:T(1,128)} %bitcast.17, bf16[4,28,48,128]{3,2,1,0:T(8,128)(2,1)} %bitcast.15, bf16[4,28,48,128]{3,2,1,0:T(8,128)(2,1)} %bitcast.16, bf16[9,28,28]{2,1,0:T(8,128)(2,1)} %w1.1, ...), custom_call_target="tpu_custom_call" | custom-call | tf_op jit(solution)/shard_map/pallas_call | solution.py:424
  5.0 14.9 %all_to_all.5.mine = bf16[32,16,128]{2,1,0:T(8,128)(2,1)S(1)} all-to-all(bf16[32,16,128]{2,1,0:T(8,128)(2,1)S(1)} %get-tuple-element.8), channel_id=1, replica_groups=mesh['segment'=4,'patch'=8] {'segment','patch'}, dimensions={0} | all-to-all | bytes 262144 | tf_op jit(solution)/shard_map/all_to_all | solution.py:493
  19.9 0.8 %shard_map.146 = f32[8,3,4,128]{3,2,1,0:T(4,128)} custom-call(bf16[128,512]{1,0:T(8,128)(2,1)S(1)} %get-tuple-element.7.adder, bf16[32,16,128]{2,1,0:T(8,128)(2,1)S(1)} %all_to_all.5.mine), custom_call_target="tpu_custom_call" | custom-call | tf_op jit(solution)/shard_map/pallas_call | solution.py:494
